TPU v7x, 32 devices: a whole 2x2x4 slice. The times are simulated.
32 devices in a mesh: gx: 8 (over y, x, core), gy: 4 (over z).
Axes of the slice: x: 2, y: 2, z: 4, core: 2. Of those that a mesh axis runs over, the one named last changes fastest.
Arguments:
- residual_in: float32 [112, 56, 336], P('gx', 'gy'), may hold values from -8 to 8
Outputs:
- correction: float32 [112, 56, 336], P('gx', 'gy')
- coarse_correction: float32 [16, 8, 48], P('gx', 'gy')
All inputs are finite; a program needn't handle non-finite values.
Results may differ from a plain program's by a relative error of at most 0.0003.
Values sent between devices are 32-bit elements; how exact they have to be, the bound alone decides.
A program may use at most 64 MiB of HBM per device.

v0:
```python
import functools
import math

import jax
import jax.numpy as jnp
import ml_dtypes
import numpy as np
from jax import lax
from jax.experimental import pallas as pl
from jax.experimental.pallas import tpu as pltpu
from jax.sharding import PartitionSpec as P

theta_cheb = 1.125
delta_cheb = 0.875
start_points = [
    -0.8717401485096066,
    -0.5917001814331423,
    -0.2092992179024789,
    0.2092992179024789,
    0.5917001814331423,
    0.8717401485096066,
]


def legendre_pair(value):
    before, now = (1.0, value)
    for order in range(1, 7):
        before, now = (now, ((2 * order + 1) * value * now - order * before) / (order + 1))
    return (now, before)


def lobatto_tables():
    point_list = [-1.0]
    for guess in start_points:
        place = guess
        for newton in range(4):
            seventh, sixth = legendre_pair(place)
            slope = 7.0 * (place * seventh - sixth) / (place * place - 1.0)
            curve = (2.0 * place * slope - 56.0 * seventh) / (1.0 - place * place)
            place = place - slope / curve
        point_list.append(place)
    point_list.append(1.0)
    sample_nodes_list = np.array(point_list)
    values = np.array([legendre_pair(place)[0] for place in point_list])
    weights = 2.0 / (56.0 * values * values)
    derivative = np.zeros((8, 8))
    for i in range(8):
        for j in range(8):
            if i != j:
                derivative[i, j] = values[i] / (
                    values[j] * (sample_nodes_list[i] - sample_nodes_list[j])
                )
    derivative[0, 0] = -14.0
    derivative[7, 7] = 14.0
    stiffness = derivative.T @ (weights[:, None] * derivative)
    return (sample_nodes_list, weights, stiffness)


def assemble(elements, stiffness, weights):
    width = 7 * elements + 1
    assembled = np.zeros((width, width))
    masses = np.zeros(width)
    for e in range(elements):
        assembled[7 * e : 7 * e + 8, 7 * e : 7 * e + 8] += stiffness
        masses[7 * e : 7 * e + 8] += weights
    return (assembled, masses)


def jacobi_eigen(matrix):
    order = matrix.shape[0]
    work = [[float(matrix[i, j]) for j in range(order)] for i in range(order)]
    vectors = [[1.0 if i == j else 0.0 for j in range(order)] for i in range(order)]
    for sweep in range(12):
        for p in range(order):
            for q in range(p + 1, order):
                angle = 0.5 * math.atan2(2.0 * work[p][q], work[q][q] - work[p][p])
                cosine = math.cos(angle)
                sine = math.sin(angle)
                for k in range(order):
                    left, right = (work[k][p], work[k][q])
                    work[k][p] = cosine * left - sine * right
                    work[k][q] = sine * left + cosine * right
                for k in range(order):
                    left, right = (work[p][k], work[q][k])
                    work[p][k] = cosine * left - sine * right
                    work[q][k] = sine * left + cosine * right
                for k in range(order):
                    left, right = (vectors[k][p], vectors[k][q])
                    vectors[k][p] = cosine * left - sine * right
                    vectors[k][q] = sine * left + cosine * right
    return (np.array([work[i][i] for i in range(order)]), np.array(vectors))


def schwarz_basis():
    sample_nodes_list, weights, stiffness = lobatto_tables()
    assembled, masses = assemble(3, stiffness, weights)
    block_stiff = assembled[6:16, 6:16]
    inv_root = 1.0 / np.sqrt(masses[6:16])
    eigen_vals, eigen_vecs = jacobi_eigen(inv_root[:, None] * block_stiff * inv_root[None, :])
    return (inv_root[:, None] * eigen_vecs, eigen_vals)


def injection_coefficients(elements, sample_nodes_list):
    matrix = np.zeros((elements + 1, 7 * elements))
    for e in range(elements):
        for m in range(7):
            matrix[e, 7 * e + m] += (1.0 - sample_nodes_list[m]) / 2.0
            matrix[e + 1, 7 * e + m] += (1.0 + sample_nodes_list[m]) / 2.0
    return matrix


MESH = pl.DeviceIdType.MESH
LANES = 64
DIRECTIONS = [(-1, 0), (1, 0), (0, -1), (0, 1), (-1, -1), (-1, 1), (1, -1), (1, 1)]


def round_up(value, unit):
    return -(-value // unit) * unit


def sine_np(vertices, elements):
    modes = np.arange(elements)
    vertex = np.asarray(vertices)[:, None]
    entries = np.sqrt(2.0 / elements) * np.sin(np.pi * (vertex * modes % (2 * elements)) / elements)
    entries = entries / np.sqrt((4.0 + 2.0 * np.cos(np.pi * modes / elements)) / 3.0)
    inside = (modes > 0) & (vertex > 0) & (vertex < elements)
    return np.where(inside, entries, 0.0)


def eigen_np(elements):
    modes = np.arange(elements)
    cosine = np.cos(np.pi * modes / elements)
    return np.where(modes > 0, 3.0 * (1.0 - cosine) / (4.0 + 2.0 * cosine), 1.0)


def split_np(matrix):
    high = matrix.astype(np.float32).astype(ml_dtypes.bfloat16)
    low = (matrix - high.astype(np.float64)).astype(np.float32).astype(ml_dtypes.bfloat16)
    return np.stack([high, low])


def pad_np(matrix, rows, columns, value=0.0):
    out = np.full((rows, columns), value)
    out[: matrix.shape[0], : matrix.shape[1]] = matrix
    return out


class Line:
    def __init__(self, elements, stiffness, weights, eigen_basis, points):
        self.elements = elements
        self.nodes = 7 * elements
        around, masses = assemble(elements + 4, stiffness, weights)
        self.around, self.masses, self.shift = around, masses, 14
        self.forward = np.zeros((10 * elements, self.nodes + 3))
        self.backward = np.zeros((self.nodes, 10 * elements))
        for e in range(elements):
            self.forward[10 * e : 10 * e + 10, 7 * e : 7 * e + 10] = eigen_basis.T
            self.backward[7 * e : 7 * e + 7, 10 * e : 10 * e + 10] = eigen_basis[1:8]
        hats = injection_coefficients(elements + 4, points)
        kept = slice(self.shift, self.shift + self.nodes)
        rows = slice(1, 1 + elements + 2)
        full = np.zeros((hats.shape[0], self.around.shape[0]))
        full[:, : hats.shape[1]] = hats
        self.hats = hats[rows, kept]
        self.hats_stiff = (full @ around)[rows, kept]
        self.hats_mass = (full * masses)[rows, kept]

    def stiff(self, i, j):
        return self.around[i + self.shift, j + self.shift]

    def mass(self, i):
        return self.masses[i + self.shift]

    def values(self, side):
        n = self.nodes
        return {-1: [-1], 0: list(range(n)), 1: [n, n + 1]}[side]

    def sums(self, side):
        n = self.nodes
        return {-1: [-1, 0], 0: [], 1: [n, n + 1]}[side]


def segments(lines, with_sums):
    line_x, line_y = lines
    out, start = [], 0
    for dx, dy in DIRECTIONS:
        rows = [("v", i, j) for i in line_x.values(dx) for j in line_y.values(dy)]
        if with_sums:
            rows += [("x", i, j) for i in line_x.sums(dx) for j in line_y.values(dy)]
            rows += [("y", i, j) for i in line_x.values(dx) for j in line_y.sums(dy)]
        size = round_up(len(rows), 8)
        out.append((start, size, rows))
        start += size
    return out, start


def tables(mesh_x, mesh_y, shape):
    points, weights, stiffness = lobatto_tables()
    eigen_basis, eigen_vals = schwarz_basis()
    nx, ny, nz = shape
    ex, ey, ez = nx // 7, ny // 7, nz // 7
    line_x = Line(ex, stiffness, weights, eigen_basis, points)
    line_y = Line(ey, stiffness, weights, eigen_basis, points)
    lines = (line_x, line_y)
    pitch = round_up(ny, 8)
    own_rows = round_up(nx * pitch, 128)
    zl = round_up(nz, 128)
    cl = round_up(10 * ez, 128)
    coefs = 100 * ex * ey
    own = lambda i, j: i * pitch + j
    own_list = [(i, j) for i in range(nx) for j in range(ny)]
    t = {}
    dims = dict(nx=nx, ny=ny, nz=nz, pitch=pitch, own_rows=own_rows, zl=zl, cl=cl, coefs=coefs)

    forward = lambda i, j: np.kron(line_x.forward[:, i + 1], line_y.forward[:, j + 1])
    seg_b, rows_b = segments(lines, False)
    seg_d, rows_d = segments(lines, True)
    dims.update(seg_b=[s[:2] for s in seg_b], rows_b=rows_b)
    dims.update(seg_d=[s[:2] for s in seg_d], rows_d=rows_d)

    pick = np.zeros((rows_b, own_rows))
    w_halo = np.zeros((coefs, rows_b))
    for (dx, dy), (start, size, rows) in zip(DIRECTIONS, seg_b):
        for r, (kind, i, j) in enumerate(rows):
            pick[start + r, own(i - nx * dx, j - ny * dy)] = 1.0
            w_halo[:, start + r] = forward(i, j)
    w_own = np.zeros((coefs, own_rows))
    back = np.zeros((own_rows, coefs))
    for i, j in own_list:
        w_own[:, own(i, j)] = forward(i, j)
        back[own(i, j)] = np.kron(line_x.backward[i], line_y.backward[j])
    t["pick"] = pick.astype(ml_dtypes.bfloat16)
    t["w_own"], t["w_halo"], t["back"] = split_np(w_own), split_np(w_halo), split_np(back)

    z_fwd = np.zeros((zl, cl))
    z_back = np.zeros((cl, zl))
    for e in range(ez):
        for m in range(10):
            z = 7 * e - 1 + m
            if 0 <= z < nz:
                z_fwd[z, 10 * e : 10 * e + 10] = eigen_basis[m]
                if 1 <= m <= 7 and z > 0:
                    z_back[10 * e : 10 * e + 10, z] = eigen_basis[m]
    t["z_fwd"], t["z_back"] = split_np(z_fwd), split_np(z_back)
    l_x, l_y = np.tile(eigen_vals, ex), np.tile(eigen_vals, ey)
    t["l_xy"] = (l_x[:, None] + l_y[None, :]).reshape(coefs, 1).astype(np.float32)
    l_z = np.ones((1, cl))
    l_z[0, : 10 * ez] = np.tile(eigen_vals, ez)
    t["l_z"] = l_z.astype(np.float32)

    send = np.zeros((rows_d, own_rows))
    wide_y = ny + 3
    points_rows = round_up((nx + 3) * wide_y, 16)
    target = lambda i, j: (i + 1) * wide_y + (j + 1)
    inside_x = lambda i: -1 <= i <= nx + 1
    inside_y = lambda j: -1 <= j <= ny + 1
    dims["points_rows"], dims["wide_y"] = points_rows, wide_y
    lap_own = np.zeros((2 * points_rows, own_rows))
    lap_halo = np.zeros((2 * points_rows, rows_d))

    def value_column(column, i, j, dx, dy):
        for k in range(-1, nx + 2):
            if k not in line_x.sums(dx):
                column[target(k, j)] += line_x.stiff(k, i) * line_y.mass(j)
        for k in range(-1, ny + 2):
            if k not in line_y.sums(dy):
                column[target(i, k)] += line_y.stiff(k, j) * line_x.mass(i)
        column[points_rows + target(i, j)] += line_x.mass(i) * line_y.mass(j)

    for i, j in own_list:
        value_column(lap_own[:, own(i, j)], i, j, 0, 0)
    for (dx, dy), (start, size, rows) in zip(DIRECTIONS, seg_d):
        for r, (kind, i, j) in enumerate(rows):
            p, q = i - nx * dx, j - ny * dy
            if kind == "v":
                send[start + r, own(p, q)] = 1.0
                value_column(lap_halo[:, start + r], i, j, dx, dy)
            elif kind == "x":
                for k in range(nx):
                    send[start + r, own(k, q)] = line_x.stiff(p, k)
                lap_halo[target(i, j), start + r] += line_y.mass(j)
            else:
                for k in range(ny):
                    send[start + r, own(p, k)] = line_y.stiff(q, k)
                lap_halo[target(i, j), start + r] += line_x.mass(i)
    w_all = np.zeros((coefs, points_rows))
    for i in range(-1, nx + 2):
        for j in range(-1, ny + 2):
            w_all[:, target(i, j)] = forward(i, j)
    t["send"], t["lap_own"], t["lap_halo"] = split_np(send), split_np(lap_own), split_np(lap_halo)
    t["w_all"] = split_np(w_all)
    stiff_z, mass_z = assemble(ez, stiffness, weights)
    stiff_z = stiff_z[:nz, :nz]
    t["stiff_z"] = split_np(pad_np(stiff_z, zl, zl))
    t["mass_z"] = pad_np(mass_z[None, :nz], 1, zl).astype(np.float32)

    count_x, count_y = mesh_x * ex, mesh_y * ey
    vx, vy = ex + 2, ey + 2
    dims.update(vy=vy, count_x=count_x, lanes=count_y * LANES)
    coarse = np.zeros((3, 8 * vy, own_rows))
    for i, j in own_list:
        for w in range(vy):
            for v in range(vx):
                row = 8 * w + v
                coarse[0, row, own(i, j)] = line_x.hats[v, i] * line_y.hats[w, j]
                coarse[1, row, own(i, j)] = (
                    line_x.hats_stiff[v, i] * line_y.hats_mass[w, j]
                    + line_x.hats_mass[v, i] * line_y.hats_stiff[w, j]
                )
                coarse[2, row, own(i, j)] = line_x.hats_mass[v, i] * line_y.hats_mass[w, j]
    t["coarse_b"] = split_np(coarse[0])
    t["coarse_x"] = split_np(np.concatenate([coarse[1], coarse[2]]))
    hats_z = injection_coefficients(ez, points)[:ez]
    phi_z = sine_np(np.arange(ez), ez)
    to_modes = pad_np(hats_z.T @ phi_z, zl, LANES)
    to_modes[0] = 0.0
    stiff_modes = pad_np(stiff_z @ to_modes[:nz, :ez], zl, LANES)
    mass_modes = to_modes
    t["to_modes"] = split_np(np.tile(mass_modes, (1, count_y)))
    t["to_modes_k"] = split_np(np.tile(stiff_modes, (1, count_y)))
    y_in = np.zeros((mesh_y, 8 * vy, count_y * LANES))
    y_out = np.zeros((mesh_y, 8 * (ey + 1), count_y * LANES))
    for p in range(mesh_y):
        y_in[p] = np.repeat(np.repeat(sine_np(p * ey - 1 + np.arange(vy), count_y), 8, 0), LANES, 1)
        y_out[p] = np.repeat(np.repeat(sine_np(p * ey + np.arange(ey + 1), count_y), 8, 0), LANES, 1)
    t["y_in"], t["y_out"] = y_in.astype(np.float32), y_out.astype(np.float32)
    x_in = np.zeros((count_x, mesh_x, 8))
    x_out = np.zeros((mesh_x, 8, count_x))
    for p in range(mesh_x):
        x_in[:, p, :vx] = sine_np(p * ex - 1 + np.arange(vx), count_x).T
        x_out[p, : ex + 1] = sine_np(p * ex + np.arange(ex + 1), count_x)
    t["x_in"] = x_in.reshape(count_x, mesh_x * 8).astype(np.float32)
    t["x_out"] = x_out.astype(np.float32)
    mu = np.ones((count_x, count_y, LANES))
    mu[:, :, :ez] = (
        eigen_np(count_x)[:, None, None] + eigen_np(count_y)[None, :, None] + eigen_np(ez)
    )
    t["mu"] = mu.reshape(count_x, count_y * LANES).astype(np.float32)
    z_out = np.zeros((LANES, zl + 128))
    z_out[:ez, :nz] = phi_z.T @ hats_z
    z_out[:, 0] = 0.0
    z_out[:ez, zl : zl + ez] = phi_z.T
    t["z_out"] = split_np(np.tile(z_out, (count_y, 1)))
    spread = np.zeros((own_rows, 8 * (ey + 1)))
    hats_x, hats_y = line_x.hats[1:], line_y.hats[1:]
    for i, j in own_list:
        for q in range(ey + 1):
            for p in range(ex + 1):
                spread[own(i, j), 8 * q + p] = hats_x[p, i] * hats_y[q, j]
    t["spread"] = split_np(spread)
    return t, dims


def halves(value):
    high = value.astype(jnp.bfloat16)
    return high, (value - high.astype(jnp.float32)).astype(jnp.bfloat16)


def mm(a, b):
    return jnp.dot(a, b, preferred_element_type=jnp.float32)


def left(table, parts):
    high, low = parts
    return mm(table[0], high) + (mm(table[0], low) + mm(table[1], high))


def right(parts, table):
    high, low = parts
    return mm(high, table[0]) + (mm(high, table[1]) + mm(low, table[0]))


def exact(a, b):
    return jnp.dot(a, b, precision=lax.Precision.HIGHEST, preferred_element_type=jnp.float32)


def kernel(names, dims, mesh_x, mesh_y, residual, *refs):
    t = dict(zip(names, refs[: len(names)]))
    (fine_out, coarse_out, own, out_b, in_b, out_d, in_d, out_y, in_y, out_x, in_x,
     sent, got, sent_y, got_y, sent_x, got_x) = refs[len(names):]
    nx, ny, nz, pitch = dims["nx"], dims["ny"], dims["nz"], dims["pitch"]
    own_rows, zl = dims["own_rows"], dims["zl"]
    ix, iy = lax.axis_index("gx"), lax.axis_index("gy")

    def exists(dx, dy):
        return (ix + dx >= 0) & (ix + dx < mesh_x) & (iy + dy >= 0) & (iy + dy < mesh_y)

    own[...] = jnp.zeros_like(own)
    in_b[...] = jnp.zeros_like(in_b)
    in_d[...] = jnp.zeros_like(in_d)
    barrier = pltpu.get_barrier_semaphore()
    for o in range(1, mesh_x):
        pl.semaphore_signal(
            barrier, inc=1, device_id=(lax.rem(ix + o, mesh_x), iy), device_id_type=MESH
        )
    for o in range(1, mesh_y):
        pl.semaphore_signal(
            barrier, inc=1, device_id=(ix, lax.rem(iy + o, mesh_y)), device_id_type=MESH
        )
    corners = DIRECTIONS[4:]
    for dx, dy in corners:
        @pl.when(exists(dx, dy))
        def _():
            pl.semaphore_signal(barrier, inc=1, device_id=(ix + dx, iy + dy), device_id_type=MESH)

    row = lax.broadcasted_iota(jnp.int32, (own_rows, 1), 0)
    node_x, node_y = ix * nx + row // pitch, iy * ny + row % pitch
    keep = ((node_x > 0) & (node_y > 0) & (row % pitch < ny) & (row // pitch < nx)).astype(
        jnp.float32
    )
    keep_z = (lax.broadcasted_iota(jnp.int32, (1, nz), 1) > 0).astype(jnp.float32)
    for i in range(nx):
        own[i * pitch : i * pitch + ny, 0:nz] = residual[i] * keep_z
    source = halves(own[...] * keep)
    out_b[...] = mm(t["pick"][...], source[0]) + mm(t["pick"][...], source[1])

    greetings = mesh_x - 1 + mesh_y - 1
    for dx, dy in corners:
        greetings = greetings + exists(dx, dy).astype(jnp.int32)
    pl.semaphore_wait(barrier, greetings)

    def halo(phase, src, dst, places):
        copies = []
        for d, (dx, dy) in enumerate(DIRECTIONS):
            start, size = places[d]
            copies.append(
                pltpu.make_async_remote_copy(
                    src_ref=src.at[pl.ds(start, size)],
                    dst_ref=dst.at[pl.ds(start, size)],
                    send_sem=sent.at[phase, d],
                    recv_sem=got.at[phase, d],
                    device_id=(ix - dx, iy - dy),
                    device_id_type=MESH,
                )
            )
        for d, (dx, dy) in enumerate(DIRECTIONS):
            pl.when(exists(-dx, -dy))(copies[d].start)
        return copies

    def arrived(copies):
        for d, (dx, dy) in enumerate(DIRECTIONS):
            pl.when(exists(dx, dy))(copies[d].wait_recv)

    def left_here(copies):
        for d, (dx, dy) in enumerate(DIRECTIONS):
            pl.when(exists(-dx, -dy))(copies[d].wait_send)

    def solve(coefs):
        modes = right(halves(coefs), t["z_fwd"])
        modes = modes / (t["l_xy"][...] + t["l_z"][...])
        modes = left(t["back"], halves(modes))
        return right(halves(modes), t["z_back"]) * keep

    copies_b = halo(0, out_b, in_b, dims["seg_b"])
    coefs = left(t["w_own"], source)
    coarse_b = left(t["coarse_b"], source)
    arrived(copies_b)
    coefs = coefs + left(t["w_halo"], halves(in_b[...]))
    first = solve(coefs) * (1.0 / theta_cheb)

    parts = halves(first)
    out_d[...] = left(t["send"], parts)
    copies_d = halo(1, out_d, in_d, dims["seg_d"])
    applied = left(t["lap_own"], parts)
    arrived(copies_d)
    applied = applied + left(t["lap_halo"], halves(in_d[...]))
    rows, wide_y = dims["points_rows"], dims["wide_y"]
    spot = lax.broadcasted_iota(jnp.int32, (rows, 1), 0)
    spot_x, spot_y = ix * nx + spot // wide_y - 1, iy * ny + spot % wide_y - 1
    inside = (spot_x > 0) & (spot_x < mesh_x * nx) & (spot_y > 0) & (spot_y < mesh_y * ny)
    lane = lax.broadcasted_iota(jnp.int32, (1, zl), 1)
    inside = (inside & (lane > 0) & (lane < nz)).astype(jnp.float32)
    applied = applied[:rows] * t["mass_z"][...] + right(halves(applied[rows:]), t["stiff_z"])
    coefs = coefs - left(t["w_all"], halves(applied * inside))
    sigma = theta_cheb / delta_cheb
    rho_0 = 1.0 / sigma
    rho_1 = 1.0 / (2.0 * sigma - rho_0)
    total = (1.0 + rho_1 * rho_0) * first + (2.0 * rho_1 / delta_cheb) * solve(coefs)

    vy = dims["vy"]
    parts = left(t["coarse_x"], halves(total))
    parts_b = coarse_b - parts[: 8 * vy] * t["mass_z"][...]
    share = right(halves(parts_b), t["to_modes"]) - right(halves(parts[8 * vy :]), t["to_modes_k"])
    share = share * t["y_in"][iy]
    share = sum(share[8 * w : 8 * w + 8] for w in range(vy))

    def everyone(value, src, dst, count, me, send_sems, recv_sems, place):
        src[...] = value
        copies = []
        for o in range(1, count):
            to = lax.rem(me + o, count)
            copies.append(
                pltpu.make_async_remote_copy(
                    src_ref=src,
                    dst_ref=dst.at[me],
                    send_sem=send_sems.at[o],
                    recv_sem=recv_sems.at[o],
                    device_id=place(to),
                    device_id_type=MESH,
                )
            )
        for copy in copies:
            copy.start()
        dst[me] = value
        for copy in copies:
            copy.wait_recv()
        return copies

    copies_y = everyone(
        share, out_y, in_y, mesh_y, iy, sent_y, got_y, lambda to: (ix, to)
    )
    share = sum(in_y[p] for p in range(mesh_y))
    copies_x = everyone(
        share, out_x, in_x, mesh_x, ix, sent_x, got_x, lambda to: (to, iy)
    )
    gathered = in_x[...].reshape(mesh_x * 8, dims["lanes"])
    modes = exact(t["x_in"][...], gathered) / t["mu"][...]
    lines = exact(t["x_out"][ix], modes)
    y_out = t["y_out"][iy]
    lines = jnp.concatenate([lines] * (y_out.shape[0] // 8), axis=0) * y_out
    nodes = right(halves(lines), t["z_out"])
    ex, ey, ez = nx // 7, ny // 7, nz // 7
    for p in range(ex):
        for q in range(ey):
            coarse_out[p, q : q + 1, :] = nodes[8 * q + p : 8 * q + p + 1, zl : zl + ez]
    result = total + left(t["spread"], halves(nodes[:, :zl])) * keep
    for i in range(nx):
        fine_out[i] = result[i * pitch : i * pitch + ny, :nz]
    left_here(copies_b)
    left_here(copies_d)
    for copy in copies_y + copies_x:
        copy.wait_send()


def per_device(mesh_x, mesh_y, residual_in):
    t, dims = tables(mesh_x, mesh_y, residual_in.shape)
    names = list(t)
    nx, ny, nz = residual_in.shape
    own_rows, zl, lanes = dims["own_rows"], dims["zl"], dims["lanes"]
    f32 = jnp.float32
    vmem = pl.BlockSpec(memory_space=pltpu.VMEM)
    return pl.pallas_call(
        functools.partial(kernel, names, dims, mesh_x, mesh_y),
        out_shape=(
            jax.ShapeDtypeStruct((nx, ny, nz), f32),
            jax.ShapeDtypeStruct((nx // 7, ny // 7, nz // 7), f32),
        ),
        in_specs=[vmem] * (1 + len(names)),
        out_specs=(vmem, vmem),
        scratch_shapes=[
            pltpu.VMEM((own_rows, zl), f32),
            pltpu.VMEM((dims["rows_b"], zl), f32),
            pltpu.VMEM((dims["rows_b"], zl), f32),
            pltpu.VMEM((dims["rows_d"], zl), f32),
            pltpu.VMEM((dims["rows_d"], zl), f32),
            pltpu.VMEM((8, lanes), f32),
            pltpu.VMEM((mesh_y, 8, lanes), f32),
            pltpu.VMEM((8, lanes), f32),
            pltpu.VMEM((mesh_x, 8, lanes), f32),
            pltpu.SemaphoreType.DMA((2, 8)),
            pltpu.SemaphoreType.DMA((2, 8)),
            pltpu.SemaphoreType.DMA((mesh_y,)),
            pltpu.SemaphoreType.DMA((mesh_y,)),
            pltpu.SemaphoreType.DMA((mesh_x,)),
            pltpu.SemaphoreType.DMA((mesh_x,)),
        ],
        compiler_params=pltpu.CompilerParams(
            collective_id=0, has_side_effects=True, vmem_limit_bytes=56 * 2**20
        ),
        cost_estimate=pl.CostEstimate(flops=10**9, bytes_accessed=10**7, transcendentals=0),
    )(residual_in, *[jnp.asarray(t[name]) for name in names])


def solution(mesh):
    return jax.shard_map(
        functools.partial(per_device, mesh.shape["gx"], mesh.shape["gy"]),
        mesh=mesh,
        in_specs=(P("gx", "gy", None),),
        out_specs=(P("gx", "gy", None), P("gx", "gy", None)),
        check_vma=False,
    )
```

profile of v0, /device:TPU:0, one launch (start us, length us, event | category | flops | bytes accessed | tf_op | source)
XLA Modules:
  0.0 36.8 jit_solution(3100713923135858098)
XLA Ops:
  0.6 33.8 %shard_map.257 = (f32[14,14,336]{2,1,0:T(8,128)}, f32[2,2,48]{2,1,0:T(2,128)}) custom-call(f32[14,14,336]{2,1,0:T(8,128)} %residual.1, bf16[128,256]{1,0:T(8,128)(2,1)} %constant.50.clone.refs_0_, bf16[2,400,256]{2,1,0:T(8,128)(2,1)} %constant.51.clone.refs_1_, bf16[2,400,128]{2,1,0:T(8,128)(2,1)} %constant.52.clone.refs_2_, ...), custom_call_target="tpu_custom_call" | custom-call | flops 1000000000 | bytes 10000000 | tf_op jit(solution)/shard_map/pallas_call | solution.py:542
  34.4 0.0 copy-start
  34.5 1.7 %copy.30 = f32[14,14,336]{2,1,0:T(8,128)} copy(f32[14,14,336]{2,1,0:T(8,128)} %get-tuple-element.4) | data formatting | bytes 526848
  36.2 0.0 copy-done
  36.2 0.6 %copy.31 = f32[2,2,48]{2,1,0:T(2,128)} copy(f32[2,2,48]{2,1,0:T(2,128)S(1)} %copy-done) | data formatting | bytes 1536
Async XLA Ops:
  34.4 1.7 %copy-start = (f32[2,2,48]{2,1,0:T(2,128)S(1)}, f32[2,2,48]{2,1,0:T(2,128)}, u32[]{:S(2)}) copy-start(f32[2,2,48]{2,1,0:T(2,128)} %get-tuple-element.5) | copy-start | bytes 2308
where the time goes:
time: 36.9 us; the launch traced here: 36.8 us
  Pallas kernels  33.8 us (92%)
  local copies, waits for them, and re-layouts  2.31 us (6%)
  between operations  0.65 us (2%)
    pallas_call x1, Pallas kernels, per_device(): pl.pallas_call(functools.partial(kernel, names, dims, mesh_x, mesh_y), ou...  33.8 us
    unnamed x4, local copies, waits for them, and re-layouts  2.31 us

commit v1 on v0

--- a/solution.py
+++ b/solution.py
@@ -133,10 +133,18 @@
     return np.where(modes > 0, 3.0 * (1.0 - cosine) / (4.0 + 2.0 * cosine), 1.0)
 
 
-def split_np(matrix):
+def split_np(matrix, axis):
     high = matrix.astype(np.float32).astype(ml_dtypes.bfloat16)
     low = (matrix - high.astype(np.float64)).astype(np.float32).astype(ml_dtypes.bfloat16)
-    return np.stack([high, low])
+    return np.concatenate([high, high, low], axis=axis)
+
+
+def lhs_np(matrix):
+    return split_np(pad_np(matrix, round_up(matrix.shape[0], 16), matrix.shape[1]), 1)
+
+
+def rhs_np(matrix):
+    return split_np(matrix, 0)
 
 
 def pad_np(matrix, rows, columns, value=0.0):
@@ -215,6 +223,7 @@
     forward = lambda i, j: np.kron(line_x.forward[:, i + 1], line_y.forward[:, j + 1])
     seg_b, rows_b = segments(lines, False)
     seg_d, rows_d = segments(lines, True)
+    rows_d = round_up(rows_d, 16)
     dims.update(seg_b=[s[:2] for s in seg_b], rows_b=rows_b)
     dims.update(seg_d=[s[:2] for s in seg_d], rows_d=rows_d)
 
@@ -229,24 +238,27 @@
     for i, j in own_list:
         w_own[:, own(i, j)] = forward(i, j)
         back[own(i, j)] = np.kron(line_x.backward[i], line_y.backward[j])
-    t["pick"] = pick.astype(ml_dtypes.bfloat16)
-    t["w_own"], t["w_halo"], t["back"] = split_np(w_own), split_np(w_halo), split_np(back)
-
     z_fwd = np.zeros((zl, cl))
     z_back = np.zeros((cl, zl))
     for e in range(ez):
         for m in range(10):
             z = 7 * e - 1 + m
-            if 0 <= z < nz:
+            if 0 < z < nz:
                 z_fwd[z, 10 * e : 10 * e + 10] = eigen_basis[m]
-                if 1 <= m <= 7 and z > 0:
+                if 1 <= m <= 7:
                     z_back[10 * e : 10 * e + 10, z] = eigen_basis[m]
-    t["z_fwd"], t["z_back"] = split_np(z_fwd), split_np(z_back)
     l_x, l_y = np.tile(eigen_vals, ex), np.tile(eigen_vals, ey)
-    t["l_xy"] = (l_x[:, None] + l_y[None, :]).reshape(coefs, 1).astype(np.float32)
-    l_z = np.ones((1, cl))
-    l_z[0, : 10 * ez] = np.tile(eigen_vals, ez)
-    t["l_z"] = l_z.astype(np.float32)
+    l_z = np.ones(cl)
+    l_z[: 10 * ez] = np.tile(eigen_vals, ez)
+    inverse = 1.0 / ((l_x[:, None] + l_y[None, :]).reshape(coefs, 1) + l_z)
+    t["z_fwd"] = rhs_np(z_fwd)
+    t["pick"] = pick.astype(ml_dtypes.bfloat16)
+    t["w_own"] = lhs_np(w_own)
+    t["coarse_b"] = None
+    t["to_modes"] = None
+    t["w_halo"] = lhs_np(w_halo)
+    t["inverse"] = inverse.astype(np.float32)
+    t["back"], t["z_back"] = lhs_np(back), rhs_np(z_back)
 
     send = np.zeros((rows_d, own_rows))
     wide_y = ny + 3
@@ -287,12 +299,12 @@
     for i in range(-1, nx + 2):
         for j in range(-1, ny + 2):
             w_all[:, target(i, j)] = forward(i, j)
-    t["send"], t["lap_own"], t["lap_halo"] = split_np(send), split_np(lap_own), split_np(lap_halo)
-    t["w_all"] = split_np(w_all)
+    t["send"], t["lap_own"], t["lap_halo"] = lhs_np(send), lhs_np(lap_own), lhs_np(lap_halo)
     stiff_z, mass_z = assemble(ez, stiffness, weights)
-    stiff_z = stiff_z[:nz, :nz]
-    t["stiff_z"] = split_np(pad_np(stiff_z, zl, zl))
-    t["mass_z"] = pad_np(mass_z[None, :nz], 1, zl).astype(np.float32)
+    stiff_z = pad_np(stiff_z[:nz, :nz], zl, zl)
+    mass_z = np.diag(pad_np(mass_z[None, :nz], 1, zl)[0])
+    t["z_lap"] = rhs_np(np.concatenate([mass_z @ z_fwd, stiff_z @ z_fwd]))
+    t["w_all"] = lhs_np(w_all)
 
     count_x, count_y = mesh_x * ex, mesh_y * ey
     vx, vy = ex + 2, ey + 2
@@ -308,16 +320,23 @@
                     + line_x.hats_mass[v, i] * line_y.hats_stiff[w, j]
                 )
                 coarse[2, row, own(i, j)] = line_x.hats_mass[v, i] * line_y.hats_mass[w, j]
-    t["coarse_b"] = split_np(coarse[0])
-    t["coarse_x"] = split_np(np.concatenate([coarse[1], coarse[2]]))
+    t["coarse_b"] = lhs_np(coarse[0])
+    coarse_m = []
+    for first_x in (0, 1):
+        for first_y in (0, 1):
+            masked = back.copy()
+            for i, j in own_list:
+                if (first_x and i == 0) or (first_y and j == 0):
+                    masked[own(i, j)] = 0.0
+            coarse_m.append(lhs_np(np.concatenate([coarse[1] @ masked, coarse[2] @ masked])))
+    t["coarse_m"] = np.stack(coarse_m)
     hats_z = injection_coefficients(ez, points)[:ez]
     phi_z = sine_np(np.arange(ez), ez)
     to_modes = pad_np(hats_z.T @ phi_z, zl, LANES)
     to_modes[0] = 0.0
-    stiff_modes = pad_np(stiff_z @ to_modes[:nz, :ez], zl, LANES)
-    mass_modes = to_modes
-    t["to_modes"] = split_np(np.tile(mass_modes, (1, count_y)))
-    t["to_modes_k"] = split_np(np.tile(stiff_modes, (1, count_y)))
+    t["to_modes"] = rhs_np(np.tile(to_modes, (1, 2)))
+    m_modes = np.concatenate([z_back @ mass_z @ to_modes, z_back @ stiff_z @ to_modes])
+    t["m_modes"] = rhs_np(np.tile(m_modes, (1, 2)))
     y_in = np.zeros((mesh_y, 8 * vy, count_y * LANES))
     y_out = np.zeros((mesh_y, 8 * (ey + 1), count_y * LANES))
     for p in range(mesh_y):
@@ -329,25 +348,25 @@
     for p in range(mesh_x):
         x_in[:, p, :vx] = sine_np(p * ex - 1 + np.arange(vx), count_x).T
         x_out[p, : ex + 1] = sine_np(p * ex + np.arange(ex + 1), count_x)
-    t["x_in"] = x_in.reshape(count_x, mesh_x * 8).astype(np.float32)
-    t["x_out"] = x_out.astype(np.float32)
+    t["x_in"] = lhs_np(x_in.reshape(count_x, mesh_x * 8))
+    t["x_out"] = np.stack([lhs_np(x_out[p]) for p in range(mesh_x)])
     mu = np.ones((count_x, count_y, LANES))
     mu[:, :, :ez] = (
         eigen_np(count_x)[:, None, None] + eigen_np(count_y)[None, :, None] + eigen_np(ez)
     )
-    t["mu"] = mu.reshape(count_x, count_y * LANES).astype(np.float32)
+    t["mu"] = (1.0 / mu).reshape(count_x, count_y * LANES).astype(np.float32)
     z_out = np.zeros((LANES, zl + 128))
     z_out[:ez, :nz] = phi_z.T @ hats_z
     z_out[:, 0] = 0.0
     z_out[:ez, zl : zl + ez] = phi_z.T
-    t["z_out"] = split_np(np.tile(z_out, (count_y, 1)))
+    t["z_out"] = rhs_np(np.tile(z_out, (2, 1)))
     spread = np.zeros((own_rows, 8 * (ey + 1)))
     hats_x, hats_y = line_x.hats[1:], line_y.hats[1:]
     for i, j in own_list:
         for q in range(ey + 1):
             for p in range(ex + 1):
                 spread[own(i, j), 8 * q + p] = hats_x[p, i] * hats_y[q, j]
-    t["spread"] = split_np(spread)
+    t["spread"] = lhs_np(spread)
     return t, dims
 
 
@@ -360,27 +379,41 @@
     return jnp.dot(a, b, preferred_element_type=jnp.float32)
 
 
-def left(table, parts):
-    high, low = parts
-    return mm(table[0], high) + (mm(table[0], low) + mm(table[1], high))
-
-
-def right(parts, table):
-    high, low = parts
-    return mm(high, table[0]) + (mm(high, table[1]) + mm(low, table[0]))
-
-
-def exact(a, b):
-    return jnp.dot(a, b, precision=lax.Precision.HIGHEST, preferred_element_type=jnp.float32)
+def left(table, value):
+    high, low = halves(value)
+    return mm(table, jnp.concatenate([high, low, high], axis=0))
+
+
+def right(value, table):
+    high, low = halves(value)
+    return mm(jnp.concatenate([high, low, high], axis=1), table)
+
+
+PER_DEVICE = ("coarse_m", "y_in", "x_out", "y_out")
 
 
 def kernel(names, dims, mesh_x, mesh_y, residual, *refs):
-    t = dict(zip(names, refs[: len(names)]))
-    (fine_out, coarse_out, own, out_b, in_b, out_d, in_d, out_y, in_y, out_x, in_x,
-     sent, got, sent_y, got_y, sent_x, got_x) = refs[len(names):]
+    count = len(names)
+    far = dict(zip(names, refs[:count]))
+    near = dict(zip(names, refs[count + 2 : 2 * count + 2]))
+    fine_out, coarse_out = refs[count : count + 2]
+    (own, out_b, in_b, out_d, in_d, out_y, in_y, out_x, in_x,
+     loaded, sent, got, sent_y, got_y, sent_x, got_x) = refs[2 * count + 2 :]
     nx, ny, nz, pitch = dims["nx"], dims["ny"], dims["nz"], dims["pitch"]
     own_rows, zl = dims["own_rows"], dims["zl"]
     ix, iy = lax.axis_index("gx"), lax.axis_index("gy")
+    start_of_grid = 2 * (ix == 0).astype(jnp.int32) + (iy == 0).astype(jnp.int32)
+    place = dict(coarse_m=start_of_grid, y_in=iy, x_out=ix, y_out=iy)
+    loads = {}
+    for n, name in enumerate(names):
+        src = far[name].at[place[name]] if name in place else far[name]
+        loads[name] = pltpu.make_async_copy(src, near[name], loaded.at[n])
+        loads[name].start()
+
+    def table(name):
+        if name in loads:
+            loads.pop(name).wait()
+        return near[name][...]
 
     def exists(dx, dy):
         return (ix + dx >= 0) & (ix + dx < mesh_x) & (iy + dy >= 0) & (iy + dy < mesh_y)
@@ -408,11 +441,12 @@
     keep = ((node_x > 0) & (node_y > 0) & (row % pitch < ny) & (row // pitch < nx)).astype(
         jnp.float32
     )
-    keep_z = (lax.broadcasted_iota(jnp.int32, (1, nz), 1) > 0).astype(jnp.float32)
     for i in range(nx):
-        own[i * pitch : i * pitch + ny, 0:nz] = residual[i] * keep_z
-    source = halves(own[...] * keep)
-    out_b[...] = mm(t["pick"][...], source[0]) + mm(t["pick"][...], source[1])
+        own[i * pitch : i * pitch + ny, 0:nz] = residual[i]
+    source = own[...] * keep
+    high, low = halves(source)
+    pick = table("pick")
+    out_b[...] = mm(pick, high) + mm(pick, low)
 
     greetings = mesh_x - 1 + mesh_y - 1
     for dx, dy in corners:
@@ -445,43 +479,38 @@
         for d, (dx, dy) in enumerate(DIRECTIONS):
             pl.when(exists(-dx, -dy))(copies[d].wait_send)
 
-    def solve(coefs):
-        modes = right(halves(coefs), t["z_fwd"])
-        modes = modes / (t["l_xy"][...] + t["l_z"][...])
-        modes = left(t["back"], halves(modes))
-        return right(halves(modes), t["z_back"]) * keep
-
     copies_b = halo(0, out_b, in_b, dims["seg_b"])
-    coefs = left(t["w_own"], source)
-    coarse_b = left(t["coarse_b"], source)
+    z_fwd = table("z_fwd")
+    coefs = left(table("w_own"), right(source, z_fwd))
+    coarse_b = right(left(table("coarse_b"), source), table("to_modes"))
     arrived(copies_b)
-    coefs = coefs + left(t["w_halo"], halves(in_b[...]))
-    first = solve(coefs) * (1.0 / theta_cheb)
-
-    parts = halves(first)
-    out_d[...] = left(t["send"], parts)
+    coefs = coefs + left(table("w_halo"), right(in_b[...], z_fwd))
+    modes_0 = coefs * table("inverse")
+    first = right(left(table("back"), modes_0), table("z_back")) * (keep * (1.0 / theta_cheb))
+
+    out_d[...] = left(table("send"), first)
     copies_d = halo(1, out_d, in_d, dims["seg_d"])
-    applied = left(t["lap_own"], parts)
-    arrived(copies_d)
-    applied = applied + left(t["lap_halo"], halves(in_d[...]))
+    applied = left(table("lap_own"), first)
     rows, wide_y = dims["points_rows"], dims["wide_y"]
     spot = lax.broadcasted_iota(jnp.int32, (rows, 1), 0)
     spot_x, spot_y = ix * nx + spot // wide_y - 1, iy * ny + spot % wide_y - 1
     inside = (spot_x > 0) & (spot_x < mesh_x * nx) & (spot_y > 0) & (spot_y < mesh_y * ny)
-    lane = lax.broadcasted_iota(jnp.int32, (1, zl), 1)
-    inside = (inside & (lane > 0) & (lane < nz)).astype(jnp.float32)
-    applied = applied[:rows] * t["mass_z"][...] + right(halves(applied[rows:]), t["stiff_z"])
-    coefs = coefs - left(t["w_all"], halves(applied * inside))
+    inside = inside.astype(jnp.float32)
+    arrived(copies_d)
+    applied = applied + left(table("lap_halo"), in_d[...])
+    applied = jnp.concatenate([applied[:rows] * inside, applied[rows:] * inside], axis=1)
+    coefs = coefs - left(table("w_all"), right(applied, table("z_lap")))
     sigma = theta_cheb / delta_cheb
     rho_0 = 1.0 / sigma
     rho_1 = 1.0 / (2.0 * sigma - rho_0)
-    total = (1.0 + rho_1 * rho_0) * first + (2.0 * rho_1 / delta_cheb) * solve(coefs)
+    weight_0, weight_1 = (1.0 + rho_1 * rho_0) / theta_cheb, 2.0 * rho_1 / delta_cheb
+    modes = weight_0 * modes_0 + weight_1 * (coefs * table("inverse"))
 
     vy = dims["vy"]
-    parts = left(t["coarse_x"], halves(total))
-    parts_b = coarse_b - parts[: 8 * vy] * t["mass_z"][...]
-    share = right(halves(parts_b), t["to_modes"]) - right(halves(parts[8 * vy :]), t["to_modes_k"])
-    share = share * t["y_in"][iy]
+    shares = left(table("coarse_m"), modes)
+    shares = jnp.concatenate([shares[: 8 * vy], shares[8 * vy :]], axis=1)
+    share = coarse_b - right(shares, table("m_modes"))
+    share = jnp.concatenate([share] * (dims["lanes"] // 128), axis=1) * table("y_in")
     share = sum(share[8 * w : 8 * w + 8] for w in range(vy))
 
     def everyone(value, src, dst, count, me, send_sems, recv_sems, place):
@@ -502,28 +531,35 @@
         for copy in copies:
             copy.start()
         dst[me] = value
+        return copies
+
+    def all_here(copies):
         for copy in copies:
             copy.wait_recv()
-        return copies
 
     copies_y = everyone(
         share, out_y, in_y, mesh_y, iy, sent_y, got_y, lambda to: (ix, to)
     )
+    total = left(table("back"), modes)
+    all_here(copies_y)
     share = sum(in_y[p] for p in range(mesh_y))
     copies_x = everyone(
         share, out_x, in_x, mesh_x, ix, sent_x, got_x, lambda to: (to, iy)
     )
+    total = right(total, table("z_back")) * keep
+    all_here(copies_x)
     gathered = in_x[...].reshape(mesh_x * 8, dims["lanes"])
-    modes = exact(t["x_in"][...], gathered) / t["mu"][...]
-    lines = exact(t["x_out"][ix], modes)
-    y_out = t["y_out"][iy]
+    scaled = left(table("x_in"), gathered) * table("mu")
+    lines = left(table("x_out"), scaled)[:8]
+    y_out = table("y_out")
     lines = jnp.concatenate([lines] * (y_out.shape[0] // 8), axis=0) * y_out
-    nodes = right(halves(lines), t["z_out"])
+    lines = sum(lines[:, 128 * b : 128 * b + 128] for b in range(dims["lanes"] // 128))
+    nodes = right(lines, table("z_out"))
     ex, ey, ez = nx // 7, ny // 7, nz // 7
     for p in range(ex):
         for q in range(ey):
             coarse_out[p, q : q + 1, :] = nodes[8 * q + p : 8 * q + p + 1, zl : zl + ez]
-    result = total + left(t["spread"], halves(nodes[:, :zl])) * keep
+    result = total + left(table("spread"), nodes[:, :zl]) * keep
     for i in range(nx):
         fine_out[i] = result[i * pitch : i * pitch + ny, :nz]
     left_here(copies_b)
@@ -545,9 +581,12 @@
             jax.ShapeDtypeStruct((nx, ny, nz), f32),
             jax.ShapeDtypeStruct((nx // 7, ny // 7, nz // 7), f32),
         ),
-        in_specs=[vmem] * (1 + len(names)),
+        in_specs=[vmem] + [pl.BlockSpec(memory_space=pl.ANY)] * len(names),
         out_specs=(vmem, vmem),
         scratch_shapes=[
+            pltpu.VMEM(t[name].shape[name in PER_DEVICE :], t[name].dtype) for name in names
+        ]
+        + [
             pltpu.VMEM((own_rows, zl), f32),
             pltpu.VMEM((dims["rows_b"], zl), f32),
             pltpu.VMEM((dims["rows_b"], zl), f32),
@@ -557,6 +596,7 @@
             pltpu.VMEM((mesh_y, 8, lanes), f32),
             pltpu.VMEM((8, lanes), f32),
             pltpu.VMEM((mesh_x, 8, lanes), f32),
+            pltpu.SemaphoreType.DMA((len(names),)),
             pltpu.SemaphoreType.DMA((2, 8)),
             pltpu.SemaphoreType.DMA((2, 8)),
             pltpu.SemaphoreType.DMA((mesh_y,)),

time: 36.9 us -> 33.5 us (0.908)
  Pallas kernels: 33.8 us -> 29.7 us
  local copies, waits for them, and re-layouts: 2.31 us -> 2.96 us
    pallas_call x1, Pallas kernels: 33.8 us -> 29.7 us  [per_device(): pl.pallas_call(functools.partial(kernel, names, dims, mesh_x, mesh_y), ou...]
    unnamed x4 -> x2, local copies, waits for them, and re-layouts: 2.31 us -> 2.96 us
where the time goes in v1:
time: 33.5 us; the launch traced here: 33.3 us
  Pallas kernels  29.7 us (89%)
  local copies, waits for them, and re-layouts  2.96 us (9%)
  between operations  0.64 us (2%)
    pallas_call x1, Pallas kernels, per_device(): pl.pallas_call(functools.partial(kernel, names, dims, mesh_x, mesh_y), ou...  29.7 us
    unnamed x2, local copies, waits for them, and re-layouts  2.96 us

profile of v1, /device:TPU:0, one launch (start us, length us, event | category | flops | bytes accessed | tf_op | source)
XLA Modules:
  0.0 33.3 jit_solution(9184589444450434125)
XLA Ops:
  0.6 29.7 %shard_map.239 = (f32[14,14,336]{2,1,0:T(8,128)}, f32[2,2,48]{2,1,0:T(2,128)}) custom-call(f32[14,14,336]{2,1,0:T(8,128)} %residual.1, bf16[1152,512]{1,0:T(8,128)(2,1)} %constant.46.clone.refs_0_, bf16[128,256]{1,0:T(8,128)(2,1)} %constant.47.clone.refs_1_, bf16[400,768]{1,0:T(8,128)(2,1)} %constant.48.clone.refs_2_, ...), custom_call_target="tpu_custom_call" | custom-call | flops 1000000000 | bytes 10000000 | tf_op jit(solution)/shard_map/pallas_call | solution.py:578
  30.4 1.7 %copy.28 = f32[14,14,336]{2,1,0:T(8,128)} copy(f32[14,14,336]{2,1,0:T(8,128)} %get-tuple-element.4) | data formatting | bytes 526848
  32.1 1.2 %copy.29 = f32[2,2,48]{2,1,0:T(2,128)} copy(f32[2,2,48]{2,1,0:T(2,128)} %get-tuple-element.5) | data formatting | bytes 1536

commit v2 on v1

--- a/solution.py
+++ b/solution.py
@@ -258,7 +258,8 @@
     t["to_modes"] = None
     t["w_halo"] = lhs_np(w_halo)
     t["inverse"] = inverse.astype(np.float32)
-    t["back"], t["z_back"] = lhs_np(back), rhs_np(z_back)
+    t["send_m"] = None
+    t["z_back"], t["back"] = rhs_np(z_back), lhs_np(back)
 
     send = np.zeros((rows_d, own_rows))
     wide_y = ny + 3
@@ -299,7 +300,16 @@
     for i in range(-1, nx + 2):
         for j in range(-1, ny + 2):
             w_all[:, target(i, j)] = forward(i, j)
-    t["send"], t["lap_own"], t["lap_halo"] = lhs_np(send), lhs_np(lap_own), lhs_np(lap_halo)
+    masked_backs = []
+    for first_x in (0, 1):
+        for first_y in (0, 1):
+            masked = back.copy()
+            for i, j in own_list:
+                if (first_x and i == 0) or (first_y and j == 0):
+                    masked[own(i, j)] = 0.0
+            masked_backs.append(masked)
+    t["send_m"] = np.stack([lhs_np(send @ masked / theta_cheb) for masked in masked_backs])
+    t["lap_own"], t["lap_halo"] = lhs_np(lap_own), lhs_np(lap_halo)
     stiff_z, mass_z = assemble(ez, stiffness, weights)
     stiff_z = pad_np(stiff_z[:nz, :nz], zl, zl)
     mass_z = np.diag(pad_np(mass_z[None, :nz], 1, zl)[0])
@@ -308,12 +318,14 @@
 
     count_x, count_y = mesh_x * ex, mesh_y * ey
     vx, vy = ex + 2, ey + 2
-    dims.update(vy=vy, count_x=count_x, lanes=count_y * LANES)
-    coarse = np.zeros((3, 8 * vy, own_rows))
+    assert vx == 4 and vy == 4 and count_y % 4 == 0
+    half_y = count_y // 2
+    dims.update(count_x=count_x, half_y=half_y, lanes=half_y * LANES)
+    coarse = np.zeros((3, 16, own_rows))
     for i, j in own_list:
         for w in range(vy):
             for v in range(vx):
-                row = 8 * w + v
+                row = 4 * w + v
                 coarse[0, row, own(i, j)] = line_x.hats[v, i] * line_y.hats[w, j]
                 coarse[1, row, own(i, j)] = (
                     line_x.hats_stiff[v, i] * line_y.hats_mass[w, j]
@@ -321,14 +333,9 @@
                 )
                 coarse[2, row, own(i, j)] = line_x.hats_mass[v, i] * line_y.hats_mass[w, j]
     t["coarse_b"] = lhs_np(coarse[0])
-    coarse_m = []
-    for first_x in (0, 1):
-        for first_y in (0, 1):
-            masked = back.copy()
-            for i, j in own_list:
-                if (first_x and i == 0) or (first_y and j == 0):
-                    masked[own(i, j)] = 0.0
-            coarse_m.append(lhs_np(np.concatenate([coarse[1] @ masked, coarse[2] @ masked])))
+    coarse_m = [
+        lhs_np(np.concatenate([coarse[1] @ masked, coarse[2] @ masked])) for masked in masked_backs
+    ]
     t["coarse_m"] = np.stack(coarse_m)
     hats_z = injection_coefficients(ez, points)[:ez]
     phi_z = sine_np(np.arange(ez), ez)
@@ -337,24 +344,32 @@
     t["to_modes"] = rhs_np(np.tile(to_modes, (1, 2)))
     m_modes = np.concatenate([z_back @ mass_z @ to_modes, z_back @ stiff_z @ to_modes])
     t["m_modes"] = rhs_np(np.tile(m_modes, (1, 2)))
-    y_in = np.zeros((mesh_y, 8 * vy, count_y * LANES))
-    y_out = np.zeros((mesh_y, 8 * (ey + 1), count_y * LANES))
+    y_in = np.zeros((mesh_y, count_y, 2, 4, 2, LANES))
+    y_out = np.zeros((mesh_y, 8, half_y * LANES))
     for p in range(mesh_y):
-        y_in[p] = np.repeat(np.repeat(sine_np(p * ey - 1 + np.arange(vy), count_y), 8, 0), LANES, 1)
-        y_out[p] = np.repeat(np.repeat(sine_np(p * ey + np.arange(ey + 1), count_y), 8, 0), LANES, 1)
-    t["y_in"], t["y_out"] = y_in.astype(np.float32), y_out.astype(np.float32)
-    x_in = np.zeros((count_x, mesh_x, 8))
-    x_out = np.zeros((mesh_x, 8, count_x))
+        inward = sine_np(p * ey - 1 + np.arange(vy), count_y)
+        outward = sine_np(p * ey + np.arange(ey + 1), count_y)
+        for w in range(vy):
+            y_in[p, :, w % 2, :, w // 2, :] = inward[w][:, None, None]
+        for q in range(ey + 1):
+            for h in range(2):
+                y_out[p, 2 * q + h] = np.repeat(outward[q, h * half_y : (h + 1) * half_y], LANES)
+    t["y_in"] = y_in.reshape(mesh_y * count_y * 8, 2 * LANES).astype(np.float32)
+    x_in = np.zeros((2, count_x, mesh_x, 2, 4))
+    x_out = np.zeros((mesh_x, 2, 8, 2, count_x))
     for p in range(mesh_x):
-        x_in[:, p, :vx] = sine_np(p * ex - 1 + np.arange(vx), count_x).T
-        x_out[p, : ex + 1] = sine_np(p * ex + np.arange(ex + 1), count_x)
-    t["x_in"] = lhs_np(x_in.reshape(count_x, mesh_x * 8))
-    t["x_out"] = np.stack([lhs_np(x_out[p]) for p in range(mesh_x)])
+        for h in range(2):
+            x_in[h, :, p, h] = sine_np(p * ex - 1 + np.arange(vx), count_x).T
+            x_out[p, h, : ex + 1, h] = sine_np(p * ex + np.arange(ex + 1), count_x)
+    t["x_in"] = lhs_np(x_in.reshape(2 * count_x, mesh_x * 8))
     mu = np.ones((count_x, count_y, LANES))
     mu[:, :, :ez] = (
         eigen_np(count_x)[:, None, None] + eigen_np(count_y)[None, :, None] + eigen_np(ez)
     )
-    t["mu"] = (1.0 / mu).reshape(count_x, count_y * LANES).astype(np.float32)
+    mu = mu.reshape(count_x, 2, half_y * LANES).transpose(1, 0, 2)
+    t["mu"] = (1.0 / mu).reshape(2 * count_x, half_y * LANES).astype(np.float32)
+    t["x_out"] = np.stack([lhs_np(x_out[p].reshape(16, 2 * count_x)) for p in range(mesh_x)])
+    t["y_out"] = y_out.astype(np.float32)
     z_out = np.zeros((LANES, zl + 128))
     z_out[:ez, :nz] = phi_z.T @ hats_z
     z_out[:, 0] = 0.0
@@ -366,8 +381,7 @@
         for q in range(ey + 1):
             for p in range(ex + 1):
                 spread[own(i, j), 8 * q + p] = hats_x[p, i] * hats_y[q, j]
-    t["spread"] = lhs_np(spread)
-    return t, dims
+    return t, dims, lhs_np(spread)
 
 
 def halves(value):
@@ -389,36 +403,22 @@
     return mm(jnp.concatenate([high, low, high], axis=1), table)
 
 
-PER_DEVICE = ("coarse_m", "y_in", "x_out", "y_out")
+PER_DEVICE = ("send_m", "coarse_m", "x_out", "y_out")
 
 
 def kernel(names, dims, mesh_x, mesh_y, residual, *refs):
     count = len(names)
     far = dict(zip(names, refs[:count]))
     near = dict(zip(names, refs[count + 2 : 2 * count + 2]))
-    fine_out, coarse_out = refs[count : count + 2]
-    (own, out_b, in_b, out_d, in_d, out_y, in_y, out_x, in_x,
-     loaded, sent, got, sent_y, got_y, sent_x, got_x) = refs[2 * count + 2 :]
+    total_out, nodes_out = refs[count : count + 2]
+    (block, own, out_b, in_b, out_d, in_d, out_y, in_y, out_x, in_x,
+     local, loaded, sent, got, sent_y, got_y, sent_x, got_x) = refs[2 * count + 2 :]
     nx, ny, nz, pitch = dims["nx"], dims["ny"], dims["nz"], dims["pitch"]
     own_rows, zl = dims["own_rows"], dims["zl"]
     ix, iy = lax.axis_index("gx"), lax.axis_index("gy")
-    start_of_grid = 2 * (ix == 0).astype(jnp.int32) + (iy == 0).astype(jnp.int32)
-    place = dict(coarse_m=start_of_grid, y_in=iy, x_out=ix, y_out=iy)
-    loads = {}
-    for n, name in enumerate(names):
-        src = far[name].at[place[name]] if name in place else far[name]
-        loads[name] = pltpu.make_async_copy(src, near[name], loaded.at[n])
-        loads[name].start()
-
-    def table(name):
-        if name in loads:
-            loads.pop(name).wait()
-        return near[name][...]
-
     def exists(dx, dy):
         return (ix + dx >= 0) & (ix + dx < mesh_x) & (iy + dy >= 0) & (iy + dy < mesh_y)
 
-    own[...] = jnp.zeros_like(own)
     in_b[...] = jnp.zeros_like(in_b)
     in_d[...] = jnp.zeros_like(in_d)
     barrier = pltpu.get_barrier_semaphore()
@@ -436,13 +436,30 @@
         def _():
             pl.semaphore_signal(barrier, inc=1, device_id=(ix + dx, iy + dy), device_id_type=MESH)
 
+    residual_in = pltpu.make_async_copy(residual, block, local.at[0])
+    residual_in.start()
+    start_of_grid = 2 * (ix == 0).astype(jnp.int32) + (iy == 0).astype(jnp.int32)
+    place = dict(send_m=start_of_grid, coarse_m=start_of_grid, x_out=ix, y_out=iy)
+    loads = {}
+    for n, name in enumerate(names):
+        src = far[name].at[place[name]] if name in place else far[name]
+        loads[name] = pltpu.make_async_copy(src, near[name], loaded.at[n])
+        loads[name].start()
+
+    def table(name):
+        if name in loads:
+            loads.pop(name).wait()
+        return near[name][...]
+
+    own[...] = jnp.zeros_like(own)
     row = lax.broadcasted_iota(jnp.int32, (own_rows, 1), 0)
     node_x, node_y = ix * nx + row // pitch, iy * ny + row % pitch
     keep = ((node_x > 0) & (node_y > 0) & (row % pitch < ny) & (row // pitch < nx)).astype(
         jnp.float32
     )
+    residual_in.wait()
     for i in range(nx):
-        own[i * pitch : i * pitch + ny, 0:nz] = residual[i]
+        own[i * pitch : i * pitch + ny, 0:nz] = block[i]
     source = own[...] * keep
     high, low = halves(source)
     pick = table("pick")
@@ -486,10 +503,9 @@
     arrived(copies_b)
     coefs = coefs + left(table("w_halo"), right(in_b[...], z_fwd))
     modes_0 = coefs * table("inverse")
+    out_d[...] = right(left(table("send_m"), modes_0), table("z_back"))
+    copies_d = halo(1, out_d, in_d, dims["seg_d"])
     first = right(left(table("back"), modes_0), table("z_back")) * (keep * (1.0 / theta_cheb))
-
-    out_d[...] = left(table("send"), first)
-    copies_d = halo(1, out_d, in_d, dims["seg_d"])
     applied = left(table("lap_own"), first)
     rows, wide_y = dims["points_rows"], dims["wide_y"]
     spot = lax.broadcasted_iota(jnp.int32, (rows, 1), 0)
@@ -506,12 +522,13 @@
     weight_0, weight_1 = (1.0 + rho_1 * rho_0) / theta_cheb, 2.0 * rho_1 / delta_cheb
     modes = weight_0 * modes_0 + weight_1 * (coefs * table("inverse"))
 
-    vy = dims["vy"]
+    lanes = dims["lanes"]
     shares = left(table("coarse_m"), modes)
-    shares = jnp.concatenate([shares[: 8 * vy], shares[8 * vy :]], axis=1)
+    shares = jnp.concatenate([shares[:16], shares[16:]], axis=1)
     share = coarse_b - right(shares, table("m_modes"))
-    share = jnp.concatenate([share] * (dims["lanes"] // 128), axis=1) * table("y_in")
-    share = sum(share[8 * w : 8 * w + 8] for w in range(vy))
+    lower_lanes = lax.broadcasted_iota(jnp.int32, (8, 128), 1) < LANES
+    lower_rows = lax.broadcasted_iota(jnp.int32, (8, 128), 0) < 4
+    share = jnp.where(lower_lanes, share[:8], share[8:])
 
     def everyone(value, src, dst, count, me, send_sems, recv_sems, place):
         src[...] = value
@@ -542,60 +559,88 @@
     )
     total = left(table("back"), modes)
     all_here(copies_y)
-    share = sum(in_y[p] for p in range(mesh_y))
+    half = dims["half_y"]
+    y_in = table("y_in").reshape(mesh_y, 2 * half * 8, 128)
+    tiles = []
+    for b in range(2 * half):
+        tile = sum(in_y[p] * y_in[p, 8 * b : 8 * b + 8] for p in range(mesh_y))
+        tile = tile + pltpu.roll(tile, LANES, 1)
+        tiles.append(tile + pltpu.roll(tile, 4, 0))
+    blocks = []
+    for b in range(0, half, 2):
+        lower = jnp.where(lower_lanes, tiles[b], tiles[b + 1])
+        upper = jnp.where(lower_lanes, tiles[half + b], tiles[half + b + 1])
+        blocks.append(jnp.where(lower_rows, lower, upper))
+    share = jnp.concatenate(blocks, axis=1)
     copies_x = everyone(
         share, out_x, in_x, mesh_x, ix, sent_x, got_x, lambda to: (to, iy)
     )
-    total = right(total, table("z_back")) * keep
+    own[...] = right(total, table("z_back")) * keep
+    total_copy = pltpu.make_async_copy(own, total_out, local.at[1])
+    total_copy.start()
     all_here(copies_x)
-    gathered = in_x[...].reshape(mesh_x * 8, dims["lanes"])
+    gathered = in_x[...].reshape(mesh_x * 8, lanes)
     scaled = left(table("x_in"), gathered) * table("mu")
-    lines = left(table("x_out"), scaled)[:8]
+    lines = left(table("x_out"), scaled)
     y_out = table("y_out")
-    lines = jnp.concatenate([lines] * (y_out.shape[0] // 8), axis=0) * y_out
-    lines = sum(lines[:, 128 * b : 128 * b + 128] for b in range(dims["lanes"] // 128))
-    nodes = right(lines, table("z_out"))
-    ex, ey, ez = nx // 7, ny // 7, nz // 7
-    for p in range(ex):
-        for q in range(ey):
-            coarse_out[p, q : q + 1, :] = nodes[8 * q + p : 8 * q + p + 1, zl : zl + ez]
-    result = total + left(table("spread"), nodes[:, :zl]) * keep
-    for i in range(nx):
-        fine_out[i] = result[i * pitch : i * pitch + ny, :nz]
+    by_row = []
+    for q in range(ny // 7 + 1):
+        line = lines[:8] * y_out[2 * q : 2 * q + 1] + lines[8:] * y_out[2 * q + 1 : 2 * q + 2]
+        by_row.append(sum(line[:, 128 * b : 128 * b + 128] for b in range(lanes // 128)))
+    nodes_out[...] = right(jnp.concatenate(by_row, axis=0), table("z_out"))
+    total_copy.wait()
     left_here(copies_b)
     left_here(copies_d)
     for copy in copies_y + copies_x:
         copy.wait_send()
 
 
+def finish(dims, spread, total, nodes, fine_out, coarse_out):
+    nx, ny, nz, pitch, zl = dims["nx"], dims["ny"], dims["nz"], dims["pitch"], dims["zl"]
+    ix, iy = lax.axis_index("gx"), lax.axis_index("gy")
+    row = lax.broadcasted_iota(jnp.int32, (dims["own_rows"], 1), 0)
+    keep = (ix * nx + row // pitch > 0) & (iy * ny + row % pitch > 0)
+    values = nodes[...]
+    for p in range(nx // 7):
+        for q in range(ny // 7):
+            line = values[8 * q + p : 8 * q + p + 1, zl : zl + nz // 7]
+            coarse_out[p, q : q + 1, :] = line
+    prolonged = left(spread[...], values[:, :zl])
+    result = total[...] + prolonged * keep.astype(jnp.float32)
+    for i in range(nx):
+        fine_out[i] = result[i * pitch : i * pitch + ny, :nz]
+
+
 def per_device(mesh_x, mesh_y, residual_in):
-    t, dims = tables(mesh_x, mesh_y, residual_in.shape)
+    t, dims, spread = tables(mesh_x, mesh_y, residual_in.shape)
     names = list(t)
     nx, ny, nz = residual_in.shape
     own_rows, zl, lanes = dims["own_rows"], dims["zl"], dims["lanes"]
     f32 = jnp.float32
     vmem = pl.BlockSpec(memory_space=pltpu.VMEM)
-    return pl.pallas_call(
+    total, nodes = pl.pallas_call(
         functools.partial(kernel, names, dims, mesh_x, mesh_y),
         out_shape=(
-            jax.ShapeDtypeStruct((nx, ny, nz), f32),
-            jax.ShapeDtypeStruct((nx // 7, ny // 7, nz // 7), f32),
+            jax.ShapeDtypeStruct((own_rows, zl), f32),
+            jax.ShapeDtypeStruct((8 * (ny // 7 + 1), zl + 128), f32),
         ),
-        in_specs=[vmem] + [pl.BlockSpec(memory_space=pl.ANY)] * len(names),
-        out_specs=(vmem, vmem),
+        in_specs=[pl.BlockSpec(memory_space=pl.ANY)] * (1 + len(names)),
+        out_specs=(pl.BlockSpec(memory_space=pl.ANY), vmem),
         scratch_shapes=[
             pltpu.VMEM(t[name].shape[name in PER_DEVICE :], t[name].dtype) for name in names
         ]
         + [
+            pltpu.VMEM((nx, ny, nz), f32),
             pltpu.VMEM((own_rows, zl), f32),
             pltpu.VMEM((dims["rows_b"], zl), f32),
             pltpu.VMEM((dims["rows_b"], zl), f32),
             pltpu.VMEM((dims["rows_d"], zl), f32),
             pltpu.VMEM((dims["rows_d"], zl), f32),
-            pltpu.VMEM((8, lanes), f32),
-            pltpu.VMEM((mesh_y, 8, lanes), f32),
+            pltpu.VMEM((8, 128), f32),
+            pltpu.VMEM((mesh_y, 8, 128), f32),
             pltpu.VMEM((8, lanes), f32),
             pltpu.VMEM((mesh_x, 8, lanes), f32),
+            pltpu.SemaphoreType.DMA((2,)),
             pltpu.SemaphoreType.DMA((len(names),)),
             pltpu.SemaphoreType.DMA((2, 8)),
             pltpu.SemaphoreType.DMA((2, 8)),
@@ -609,6 +654,17 @@
         ),
         cost_estimate=pl.CostEstimate(flops=10**9, bytes_accessed=10**7, transcendentals=0),
     )(residual_in, *[jnp.asarray(t[name]) for name in names])
+    return pl.pallas_call(
+        functools.partial(finish, dims),
+        out_shape=(
+            jax.ShapeDtypeStruct((nx, ny, nz), f32),
+            jax.ShapeDtypeStruct((nx // 7, ny // 7, nz // 7), f32),
+        ),
+        in_specs=[vmem] * 3,
+        out_specs=(vmem, vmem),
+        compiler_params=pltpu.CompilerParams(vmem_limit_bytes=8 * 2**20),
+        cost_estimate=pl.CostEstimate(flops=10**7, bytes_accessed=10**6, transcendentals=0),
+    )(jnp.asarray(spread), total, nodes)
 
 
 def solution(mesh):

time: 33.5 us -> 34.4 us (1.027)
  Pallas kernels: 29.7 us -> 31.8 us
  local copies, waits for them, and re-layouts: 2.96 us -> 1.79 us
    unnamed x2 -> x6, local copies, waits for them, and re-layouts: 2.96 us -> 1.79 us
    pallas_call x1, Pallas kernels: 29.7 us -> 30.8 us  [per_device(): pl.pallas_call(functools.partial(kernel, names, dims, mesh_x, mesh_y), ou...]
    pallas_call x0 -> x1, Pallas kernels: none -> 0.93 us  [per_device(): pl.pallas_call(functools.partial(finish, dims), out_shape=(jax.ShapeDtype...]
where the time goes in v2:
time: 34.4 us; the launch traced here: 34.2 us
  Pallas kernels  31.8 us (92%)
  local copies, waits for them, and re-layouts  1.79 us (5%)
  between operations  0.66 us (2%)
    pallas_call x1, Pallas kernels, per_device(): pl.pallas_call(functools.partial(kernel, names, dims, mesh_x, mesh_y), ou...  30.8 us
    unnamed x6, local copies, waits for them, and re-layouts  1.79 us
    pallas_call x1, Pallas kernels, per_device(): pl.pallas_call(functools.partial(finish, dims), out_shape=(jax.ShapeDtype...  0.93 us

profile of v2, /device:TPU:0, one launch (start us, length us, event | category | flops | bytes accessed | tf_op | source)
XLA Modules:
  0.0 34.2 jit_solution(1496314469806085439)
XLA Ops:
  0.6 0.0 copy-start.1
  0.6 30.8 %shard_map.239 = (f32[256,384]{1,0:T(8,128)}, f32[24,512]{1,0:T(8,128)}) custom-call(f32[14,14,336]{2,1,0:T(8,128)} %residual.1, bf16[1152,512]{1,0:T(8,128)(2,1)} %constant.46.clone.refs_0_, bf16[128,256]{1,0:T(8,128)(2,1)} %constant.47.clone.refs_1_, bf16[400,768]{1,0:T(8,128)(2,1)} %constant.48.clone.refs_2_, bf16[16,768]{1,0:T(8,128)(2,1)} %constant.49.clone.refs_3_, ...), custom_call_target="tpu_custom_call" | custom-call | flops 1000000000 | bytes 10000000 | tf_op jit(solution)/shard_map/pallas_call | solution.py:621
  31.5 0.0 copy-done.1
  31.5 0.0 copy-start
  31.5 1.0 %copy-done = f32[256,384]{1,0:T(8,128)S(1)} copy-done((f32[256,384]{1,0:T(8,128)S(1)}, f32[256,384]{1,0:T(8,128)}, u32[]{:S(2)}) %copy-start) | copy-done | bytes 393240
  32.5 0.0 copy-start.2
  32.5 0.8 %copy-done.2 = f32[24,512]{1,0:T(8,128)S(1)} copy-done((f32[24,512]{1,0:T(8,128)S(1)}, f32[24,512]{1,0:T(8,128)}, u32[]{:S(2)}) %copy-start.2) | copy-done | bytes 49176
  33.3 0.9 %shard_map.240 = (f32[14,14,336]{2,1,0:T(8,128)}, f32[2,2,48]{2,1,0:T(2,128)}) custom-call(bf16[256,72]{1,0:T(8,128)(2,1)S(1)} %copy-done.1, f32[256,384]{1,0:T(8,128)S(1)} %copy-done, f32[24,512]{1,0:T(8,128)S(1)} %copy-done.2), custom_call_target="tpu_custom_call" | custom-call | flops 10000000 | bytes 1000000 | tf_op jit(solution)/shard_map/pallas_call | solution.py:657
Async XLA Ops:
  0.6 30.9 %copy-start.1 = (bf16[256,72]{1,0:T(8,128)(2,1)S(1)}, bf16[256,72]{1,0:T(8,128)(2,1)}, u32[]{:S(2)}) copy-start(bf16[256,72]{1,0:T(8,128)(2,1)} %constant.68.clone.spread) | copy-start | bytes 110596
  31.5 1.0 %copy-start = (f32[256,384]{1,0:T(8,128)S(1)}, f32[256,384]{1,0:T(8,128)}, u32[]{:S(2)}) copy-start(f32[256,384]{1,0:T(8,128)} %get-tuple-element.4.total) | copy-start | bytes 1179652
  32.5 0.8 %copy-start.2 = (f32[24,512]{1,0:T(8,128)S(1)}, f32[24,512]{1,0:T(8,128)}, u32[]{:S(2)}) copy-start(f32[24,512]{1,0:T(8,128)} %get-tuple-element.5.nodes) | copy-start | bytes 147460

commit v3 on v2

--- a/solution.py
+++ b/solution.py
@@ -211,14 +211,17 @@
     line_y = Line(ey, stiffness, weights, eigen_basis, points)
     lines = (line_x, line_y)
     pitch = round_up(ny, 8)
-    own_rows = round_up(nx * pitch, 128)
+    own_rows = round_up(nx * pitch, 16)
     zl = round_up(nz, 128)
-    cl = round_up(10 * ez, 128)
+    half_z = ez // 2
+    assert ez % 2 == 0 and 10 * half_z <= 256 and zl >= 256
+    cl = 512
+    windows = [0, zl - 256]
     coefs = 100 * ex * ey
     own = lambda i, j: i * pitch + j
     own_list = [(i, j) for i in range(nx) for j in range(ny)]
     t = {}
-    dims = dict(nx=nx, ny=ny, nz=nz, pitch=pitch, own_rows=own_rows, zl=zl, cl=cl, coefs=coefs)
+    dims = dict(nx=nx, ny=ny, nz=nz, pitch=pitch, own_rows=own_rows, zl=zl, windows=windows)
 
     forward = lambda i, j: np.kron(line_x.forward[:, i + 1], line_y.forward[:, j + 1])
     seg_b, rows_b = segments(lines, False)
@@ -240,18 +243,25 @@
         back[own(i, j)] = np.kron(line_x.backward[i], line_y.backward[j])
     z_fwd = np.zeros((zl, cl))
     z_back = np.zeros((cl, zl))
+    l_z = np.ones(cl)
     for e in range(ez):
+        lane = 256 * (e // half_z) + 10 * (e % half_z)
+        l_z[lane : lane + 10] = eigen_vals
         for m in range(10):
             z = 7 * e - 1 + m
             if 0 < z < nz:
-                z_fwd[z, 10 * e : 10 * e + 10] = eigen_basis[m]
+                z_fwd[z, lane : lane + 10] = eigen_basis[m]
                 if 1 <= m <= 7:
-                    z_back[10 * e : 10 * e + 10, z] = eigen_basis[m]
+                    z_back[lane : lane + 10, z] = eigen_basis[m]
     l_x, l_y = np.tile(eigen_vals, ex), np.tile(eigen_vals, ey)
-    l_z = np.ones(cl)
-    l_z[: 10 * ez] = np.tile(eigen_vals, ez)
     inverse = 1.0 / ((l_x[:, None] + l_y[None, :]).reshape(coefs, 1) + l_z)
-    t["z_fwd"] = rhs_np(z_fwd)
+
+    def window(matrix, c):
+        kept = matrix[windows[c] : windows[c] + 256, 256 * c : 256 * c + 256]
+        assert np.count_nonzero(kept) == np.count_nonzero(matrix[:, 256 * c : 256 * c + 256])
+        return kept
+
+    t["z_fwd"] = np.stack([rhs_np(window(z_fwd, c)) for c in range(2)])
     t["pick"] = pick.astype(ml_dtypes.bfloat16)
     t["w_own"] = lhs_np(w_own)
     t["coarse_b"] = None
@@ -259,7 +269,8 @@
     t["w_halo"] = lhs_np(w_halo)
     t["inverse"] = inverse.astype(np.float32)
     t["send_m"] = None
-    t["z_back"], t["back"] = rhs_np(z_back), lhs_np(back)
+    t["z_back"] = np.stack([rhs_np(window(z_back.T, c).T) for c in range(2)])
+    t["back"] = lhs_np(back)
 
     send = np.zeros((rows_d, own_rows))
     wide_y = ny + 3
@@ -313,7 +324,10 @@
     stiff_z, mass_z = assemble(ez, stiffness, weights)
     stiff_z = pad_np(stiff_z[:nz, :nz], zl, zl)
     mass_z = np.diag(pad_np(mass_z[None, :nz], 1, zl)[0])
-    t["z_lap"] = rhs_np(np.concatenate([mass_z @ z_fwd, stiff_z @ z_fwd]))
+    both_z = [mass_z @ z_fwd, stiff_z @ z_fwd]
+    t["z_lap"] = np.stack(
+        [rhs_np(np.concatenate([window(matrix, c) for matrix in both_z])) for c in range(2)]
+    )
     t["w_all"] = lhs_np(w_all)
 
     count_x, count_y = mesh_x * ex, mesh_y * ey
@@ -403,6 +417,26 @@
     return mm(jnp.concatenate([high, low, high], axis=1), table)
 
 
+def to_coefs(values, table, windows):
+    parts = [halves(value) for value in values]
+    out = []
+    for c, start in enumerate(windows):
+        high = [part[0][:, start : start + 256] for part in parts]
+        low = [part[1][:, start : start + 256] for part in parts]
+        out.append(mm(jnp.concatenate(high + low + high, axis=1), table[c]))
+    return jnp.concatenate(out, axis=1)
+
+
+def from_coefs(value, table, windows, zl):
+    total = None
+    for c, start in enumerate(windows):
+        part = right(value[:, 256 * c : 256 * c + 256], table[c])
+        sides = [jnp.zeros((part.shape[0], n), part.dtype) for n in (start, zl - start - 256) if n]
+        part = jnp.concatenate([part] + sides if start == 0 else sides + [part], axis=1)
+        total = part if total is None else total + part
+    return total
+
+
 PER_DEVICE = ("send_m", "coarse_m", "x_out", "y_out")
 
 
@@ -414,7 +448,7 @@
     (block, own, out_b, in_b, out_d, in_d, out_y, in_y, out_x, in_x,
      local, loaded, sent, got, sent_y, got_y, sent_x, got_x) = refs[2 * count + 2 :]
     nx, ny, nz, pitch = dims["nx"], dims["ny"], dims["nz"], dims["pitch"]
-    own_rows, zl = dims["own_rows"], dims["zl"]
+    own_rows, zl, windows = dims["own_rows"], dims["zl"], dims["windows"]
     ix, iy = lax.axis_index("gx"), lax.axis_index("gy")
     def exists(dx, dy):
         return (ix + dx >= 0) & (ix + dx < mesh_x) & (iy + dy >= 0) & (iy + dy < mesh_y)
@@ -444,6 +478,9 @@
     for n, name in enumerate(names):
         src = far[name].at[place[name]] if name in place else far[name]
         loads[name] = pltpu.make_async_copy(src, near[name], loaded.at[n])
+
+    later = names.index("back")
+    for name in names[:later]:
         loads[name].start()
 
     def table(name):
@@ -497,15 +534,19 @@
             pl.when(exists(-dx, -dy))(copies[d].wait_send)
 
     copies_b = halo(0, out_b, in_b, dims["seg_b"])
+    for name in names[later:]:
+        loads[name].start()
     z_fwd = table("z_fwd")
-    coefs = left(table("w_own"), right(source, z_fwd))
+    coefs = left(table("w_own"), to_coefs([source], z_fwd, windows))
     coarse_b = right(left(table("coarse_b"), source), table("to_modes"))
     arrived(copies_b)
-    coefs = coefs + left(table("w_halo"), right(in_b[...], z_fwd))
+    coefs = coefs + left(table("w_halo"), to_coefs([in_b[...]], z_fwd, windows))
     modes_0 = coefs * table("inverse")
-    out_d[...] = right(left(table("send_m"), modes_0), table("z_back"))
+    z_back = table("z_back")
+    out_d[...] = from_coefs(left(table("send_m"), modes_0), z_back, windows, zl)
     copies_d = halo(1, out_d, in_d, dims["seg_d"])
-    first = right(left(table("back"), modes_0), table("z_back")) * (keep * (1.0 / theta_cheb))
+    first = from_coefs(left(table("back"), modes_0), z_back, windows, zl)
+    first = first * (keep * (1.0 / theta_cheb))
     applied = left(table("lap_own"), first)
     rows, wide_y = dims["points_rows"], dims["wide_y"]
     spot = lax.broadcasted_iota(jnp.int32, (rows, 1), 0)
@@ -514,8 +555,8 @@
     inside = inside.astype(jnp.float32)
     arrived(copies_d)
     applied = applied + left(table("lap_halo"), in_d[...])
-    applied = jnp.concatenate([applied[:rows] * inside, applied[rows:] * inside], axis=1)
-    coefs = coefs - left(table("w_all"), right(applied, table("z_lap")))
+    applied = [applied[:rows] * inside, applied[rows:] * inside]
+    coefs = coefs - left(table("w_all"), to_coefs(applied, table("z_lap"), windows))
     sigma = theta_cheb / delta_cheb
     rho_0 = 1.0 / sigma
     rho_1 = 1.0 / (2.0 * sigma - rho_0)
@@ -575,7 +616,7 @@
     copies_x = everyone(
         share, out_x, in_x, mesh_x, ix, sent_x, got_x, lambda to: (to, iy)
     )
-    own[...] = right(total, table("z_back")) * keep
+    own[...] = from_coefs(total, z_back, windows, zl) * keep
     total_copy = pltpu.make_async_copy(own, total_out, local.at[1])
     total_copy.start()
     all_here(copies_x)
@@ -662,7 +703,7 @@
         ),
         in_specs=[vmem] * 3,
         out_specs=(vmem, vmem),
-        compiler_params=pltpu.CompilerParams(vmem_limit_bytes=8 * 2**20),
+        compiler_params=pltpu.CompilerParams(vmem_limit_bytes=56 * 2**20),
         cost_estimate=pl.CostEstimate(flops=10**7, bytes_accessed=10**6, transcendentals=0),
     )(jnp.asarray(spread), total, nodes)
 

time: 34.4 us -> 30.7 us (0.89)
  Pallas kernels: 31.8 us -> 29.9 us
  local copies, waits for them, and re-layouts: 1.79 us -> 0 us
    pallas_call x1, Pallas kernels: 30.8 us -> 28 us  [per_device(): pl.pallas_call(functools.partial(kernel, names, dims, mesh_x, mesh_y), ou...]
    unnamed x6 -> x0, local copies, waits for them, and re-layouts: 1.79 us -> none
    pallas_call x1, Pallas kernels: 0.93 us -> 1.9 us  [per_device(): pl.pallas_call(functools.partial(finish, dims), out_shape=(jax.ShapeDtype...]
where the time goes in v3:
time: 30.7 us; the launch traced here: 30.5 us
  Pallas kernels  29.9 us (97%)
  between operations  0.64 us (2%)
    pallas_call x1, Pallas kernels, per_device(): pl.pallas_call(functools.partial(kernel, names, dims, mesh_x, mesh_y), ou...  28 us
    pallas_call x1, Pallas kernels, per_device(): pl.pallas_call(functools.partial(finish, dims), out_shape=(jax.ShapeDtype...  1.9 us

profile of v3, /device:TPU:0, one launch (start us, length us, event | category | flops | bytes accessed | tf_op | source)
XLA Modules:
  0.0 30.5 jit_solution(8682125315856371066)
XLA Ops:
  0.6 28.0 %shard_map.239 = (f32[224,384]{1,0:T(8,128)}, f32[24,512]{1,0:T(8,128)}) custom-call(f32[14,14,336]{2,1,0:T(8,128)} %residual.1, bf16[2,768,256]{2,1,0:T(8,128)(2,1)} %constant.46.clone.refs_0_, bf16[128,224]{1,0:T(8,128)(2,1)} %constant.47.clone.refs_1_, bf16[400,672]{1,0:T(8,128)(2,1)} %constant.48.clone.refs_2_, bf16[16,672]{1,0:T(8,128)(2,1)} %constant.49.clone.refs_3_, ...), custom_call_target="tpu_custom_call" | custom-call | flops 1000000000 | bytes 10000000 | tf_op jit(solution)/shard_map/pallas_call | solution.py:662
  28.6 1.9 %shard_map.240 = (f32[14,14,336]{2,1,0:T(8,128)}, f32[2,2,48]{2,1,0:T(2,128)}) custom-call(bf16[224,72]{1,0:T(8,128)(2,1)} %constant.68.clone.spread, f32[224,384]{1,0:T(8,128)} %get-tuple-element.4.total, f32[24,512]{1,0:T(8,128)} %get-tuple-element.5.nodes), custom_call_target="tpu_custom_call" | custom-call | flops 10000000 | bytes 1000000 | tf_op jit(solution)/shard_map/pallas_call | solution.py:698

commit v4 on v3

--- a/solution.py
+++ b/solution.py
@@ -278,7 +278,6 @@
     target = lambda i, j: (i + 1) * wide_y + (j + 1)
     inside_x = lambda i: -1 <= i <= nx + 1
     inside_y = lambda j: -1 <= j <= ny + 1
-    dims["points_rows"], dims["wide_y"] = points_rows, wide_y
     lap_own = np.zeros((2 * points_rows, own_rows))
     lap_halo = np.zeros((2 * points_rows, rows_d))
 
@@ -320,15 +319,28 @@
                     masked[own(i, j)] = 0.0
             masked_backs.append(masked)
     t["send_m"] = np.stack([lhs_np(send @ masked / theta_cheb) for masked in masked_backs])
-    t["lap_own"], t["lap_halo"] = lhs_np(lap_own), lhs_np(lap_halo)
     stiff_z, mass_z = assemble(ez, stiffness, weights)
     stiff_z = pad_np(stiff_z[:nz, :nz], zl, zl)
     mass_z = np.diag(pad_np(mass_z[None, :nz], 1, zl)[0])
     both_z = [mass_z @ z_fwd, stiff_z @ z_fwd]
     t["z_lap"] = np.stack(
-        [rhs_np(np.concatenate([window(matrix, c) for matrix in both_z])) for c in range(2)]
+        [rhs_np(np.concatenate([window(matrix, c) for matrix in both_z], 1)) for c in range(2)]
     )
-    t["w_all"] = lhs_np(w_all)
+    t["lap_own"], t["lap_halo"] = [], []
+    for place_x in range(3):
+        for place_y in range(3):
+            inner = np.zeros(points_rows)
+            for i in range(-1, nx + 2):
+                for j in range(-1, ny + 2):
+                    out_x = (place_x == 0 and i <= 0) or (place_x == 2 and i >= nx)
+                    out_y = (place_y == 0 and j <= 0) or (place_y == 2 and j >= ny)
+                    inner[target(i, j)] = 0.0 if out_x or out_y else 1.0
+            masked = w_all * inner
+            for name, lap in (("lap_own", lap_own), ("lap_halo", lap_halo)):
+                pair = [masked @ lap[:points_rows], masked @ lap[points_rows:]]
+                pair = np.concatenate(pair, 1)
+                t[name].append(lhs_np(pair)[:, pair.shape[1] :])
+    t["lap_own"], t["lap_halo"] = np.stack(t["lap_own"]), np.stack(t["lap_halo"])
 
     count_x, count_y = mesh_x * ex, mesh_y * ey
     vx, vy = ex + 2, ey + 2
@@ -412,19 +424,28 @@
     return mm(table, jnp.concatenate([high, low, high], axis=0))
 
 
+def left_two(table, value):
+    high, low = halves(value)
+    both = mm(table, jnp.concatenate([high, high], axis=0))
+    return both + mm(table[:, : value.shape[0]], low)
+
+
 def right(value, table):
     high, low = halves(value)
     return mm(jnp.concatenate([high, low, high], axis=1), table)
 
 
-def to_coefs(values, table, windows):
-    parts = [halves(value) for value in values]
+def to_coefs(value, table, windows):
+    high, low = halves(value)
     out = []
     for c, start in enumerate(windows):
-        high = [part[0][:, start : start + 256] for part in parts]
-        low = [part[1][:, start : start + 256] for part in parts]
-        out.append(mm(jnp.concatenate(high + low + high, axis=1), table[c]))
-    return jnp.concatenate(out, axis=1)
+        near = slice(start, start + 256)
+        out.append(mm(jnp.concatenate([high[:, near], low[:, near], high[:, near]], 1), table[c]))
+    count = out[0].shape[1] // 256
+    rows = [
+        jnp.concatenate([part[:, 256 * n : 256 * n + 256] for part in out], 1) for n in range(count)
+    ]
+    return rows[0] if count == 1 else jnp.concatenate(rows, 0)
 
 
 def from_coefs(value, table, windows, zl):
@@ -437,7 +458,7 @@
     return total
 
 
-PER_DEVICE = ("send_m", "coarse_m", "x_out", "y_out")
+PER_DEVICE = ("send_m", "lap_own", "lap_halo", "coarse_m", "x_out", "y_out")
 
 
 def kernel(names, dims, mesh_x, mesh_y, residual, *refs):
@@ -473,7 +494,11 @@
     residual_in = pltpu.make_async_copy(residual, block, local.at[0])
     residual_in.start()
     start_of_grid = 2 * (ix == 0).astype(jnp.int32) + (iy == 0).astype(jnp.int32)
-    place = dict(send_m=start_of_grid, coarse_m=start_of_grid, x_out=ix, y_out=iy)
+    place_x = 1 - (ix == 0).astype(jnp.int32) + (ix == mesh_x - 1).astype(jnp.int32)
+    place_y = 1 - (iy == 0).astype(jnp.int32) + (iy == mesh_y - 1).astype(jnp.int32)
+    in_grid = 3 * place_x + place_y
+    place = dict(send_m=start_of_grid, lap_own=in_grid, lap_halo=in_grid)
+    place.update(coarse_m=start_of_grid, x_out=ix, y_out=iy)
     loads = {}
     for n, name in enumerate(names):
         src = far[name].at[place[name]] if name in place else far[name]
@@ -521,7 +546,8 @@
                     device_id_type=MESH,
                 )
             )
-        for d, (dx, dy) in enumerate(DIRECTIONS):
+        for d in (2, 3, 4, 5, 6, 7, 0, 1):
+            dx, dy = DIRECTIONS[d]
             pl.when(exists(-dx, -dy))(copies[d].start)
         return copies
 
@@ -537,26 +563,20 @@
     for name in names[later:]:
         loads[name].start()
     z_fwd = table("z_fwd")
-    coefs = left(table("w_own"), to_coefs([source], z_fwd, windows))
+    coefs = left(table("w_own"), to_coefs(source, z_fwd, windows))
     coarse_b = right(left(table("coarse_b"), source), table("to_modes"))
     arrived(copies_b)
-    coefs = coefs + left(table("w_halo"), to_coefs([in_b[...]], z_fwd, windows))
+    coefs = coefs + left(table("w_halo"), to_coefs(in_b[...], z_fwd, windows))
     modes_0 = coefs * table("inverse")
     z_back = table("z_back")
     out_d[...] = from_coefs(left(table("send_m"), modes_0), z_back, windows, zl)
     copies_d = halo(1, out_d, in_d, dims["seg_d"])
     first = from_coefs(left(table("back"), modes_0), z_back, windows, zl)
     first = first * (keep * (1.0 / theta_cheb))
-    applied = left(table("lap_own"), first)
-    rows, wide_y = dims["points_rows"], dims["wide_y"]
-    spot = lax.broadcasted_iota(jnp.int32, (rows, 1), 0)
-    spot_x, spot_y = ix * nx + spot // wide_y - 1, iy * ny + spot % wide_y - 1
-    inside = (spot_x > 0) & (spot_x < mesh_x * nx) & (spot_y > 0) & (spot_y < mesh_y * ny)
-    inside = inside.astype(jnp.float32)
+    z_lap = table("z_lap")
+    coefs = coefs - left_two(table("lap_own"), to_coefs(first, z_lap, windows))
     arrived(copies_d)
-    applied = applied + left(table("lap_halo"), in_d[...])
-    applied = [applied[:rows] * inside, applied[rows:] * inside]
-    coefs = coefs - left(table("w_all"), to_coefs(applied, table("z_lap"), windows))
+    coefs = coefs - left_two(table("lap_halo"), to_coefs(in_d[...], z_lap, windows))
     sigma = theta_cheb / delta_cheb
     rho_0 = 1.0 / sigma
     rho_1 = 1.0 / (2.0 * sigma - rho_0)

time: 30.7 us -> 29.8 us (0.971)
  Pallas kernels: 29.9 us -> 29 us
    pallas_call x1, Pallas kernels: 28 us -> 27.1 us  [per_device(): pl.pallas_call(functools.partial(kernel, names, dims, mesh_x, mesh_y), ou...]
where the time goes in v4:
time: 29.8 us; the launch traced here: 29.6 us
  Pallas kernels  29 us (97%)
  between operations  0.64 us (2%)
    pallas_call x1, Pallas kernels, per_device(): pl.pallas_call(functools.partial(kernel, names, dims, mesh_x, mesh_y), ou...  27.1 us
    pallas_call x1, Pallas kernels, per_device(): pl.pallas_call(functools.partial(finish, dims), out_shape=(jax.ShapeDtype...  1.9 us

profile of v4, /device:TPU:0, one launch (start us, length us, event | category | flops | bytes accessed | tf_op | source)
XLA Modules:
  0.0 29.6 jit_solution(8753942649610414072)
XLA Ops:
  0.6 27.1 %shard_map.230 = (f32[224,384]{1,0:T(8,128)}, f32[24,512]{1,0:T(8,128)}) custom-call(f32[14,14,336]{2,1,0:T(8,128)} %residual.1, bf16[2,768,256]{2,1,0:T(8,128)(2,1)} %constant.44.clone.refs_0_, bf16[128,224]{1,0:T(8,128)(2,1)} %constant.45.clone.refs_1_, bf16[400,672]{1,0:T(8,128)(2,1)} %constant.46.clone.refs_2_, bf16[16,672]{1,0:T(8,128)(2,1)} %constant.47.clone.refs_3_, ...), custom_call_target="tpu_custom_call" | custom-call | flops 1000000000 | bytes 10000000 | tf_op jit(solution)/shard_map/pallas_call | solution.py:682
  27.7 1.9 %shard_map.231 = (f32[14,14,336]{2,1,0:T(8,128)}, f32[2,2,48]{2,1,0:T(2,128)}) custom-call(bf16[224,72]{1,0:T(8,128)(2,1)} %constant.65.clone.spread, f32[224,384]{1,0:T(8,128)} %get-tuple-element.4.total, f32[24,512]{1,0:T(8,128)} %get-tuple-element.5.nodes), custom_call_target="tpu_custom_call" | custom-call | flops 10000000 | bytes 1000000 | tf_op jit(solution)/shard_map/pallas_call | solution.py:718

commit v5 on v4

--- a/solution.py
+++ b/solution.py
@@ -261,8 +261,8 @@
         assert np.count_nonzero(kept) == np.count_nonzero(matrix[:, 256 * c : 256 * c + 256])
         return kept
 
+    t["pick"] = pick.astype(ml_dtypes.bfloat16)
     t["z_fwd"] = np.stack([rhs_np(window(z_fwd, c)) for c in range(2)])
-    t["pick"] = pick.astype(ml_dtypes.bfloat16)
     t["w_own"] = lhs_np(w_own)
     t["coarse_b"] = None
     t["to_modes"] = None
@@ -474,6 +474,8 @@
     def exists(dx, dy):
         return (ix + dx >= 0) & (ix + dx < mesh_x) & (iy + dy >= 0) & (iy + dy < mesh_y)
 
+    residual_in = pltpu.make_async_copy(residual, block, local.at[0])
+    residual_in.start()
     in_b[...] = jnp.zeros_like(in_b)
     in_d[...] = jnp.zeros_like(in_d)
     barrier = pltpu.get_barrier_semaphore()
@@ -491,9 +493,8 @@
         def _():
             pl.semaphore_signal(barrier, inc=1, device_id=(ix + dx, iy + dy), device_id_type=MESH)
 
-    residual_in = pltpu.make_async_copy(residual, block, local.at[0])
-    residual_in.start()
     start_of_grid = 2 * (ix == 0).astype(jnp.int32) + (iy == 0).astype(jnp.int32)
+    own[...] = jnp.zeros_like(own)
     place_x = 1 - (ix == 0).astype(jnp.int32) + (ix == mesh_x - 1).astype(jnp.int32)
     place_y = 1 - (iy == 0).astype(jnp.int32) + (iy == mesh_y - 1).astype(jnp.int32)
     in_grid = 3 * place_x + place_y
@@ -513,7 +514,6 @@
             loads.pop(name).wait()
         return near[name][...]
 
-    own[...] = jnp.zeros_like(own)
     row = lax.broadcasted_iota(jnp.int32, (own_rows, 1), 0)
     node_x, node_y = ix * nx + row // pitch, iy * ny + row % pitch
     keep = ((node_x > 0) & (node_y > 0) & (row % pitch < ny) & (row // pitch < nx)).astype(

time: 29.8 us -> 28.8 us (0.966)
  Pallas kernels: 29 us -> 28 us
    pallas_call x1, Pallas kernels: 27.1 us -> 26.1 us  [per_device(): pl.pallas_call(functools.partial(kernel, names, dims, mesh_x, mesh_y), ou...]
where the time goes in v5:
time: 28.8 us; the launch traced here: 28.6 us
  Pallas kernels  28 us (97%)
  between operations  0.64 us (2%)
    pallas_call x1, Pallas kernels, per_device(): pl.pallas_call(functools.partial(kernel, names, dims, mesh_x, mesh_y), ou...  26.1 us
    pallas_call x1, Pallas kernels, per_device(): pl.pallas_call(functools.partial(finish, dims), out_shape=(jax.ShapeDtype...  1.91 us

profile of v5, /device:TPU:0, one launch (start us, length us, event | category | flops | bytes accessed | tf_op | source)
XLA Modules:
  0.0 28.6 jit_solution(11133207471974721556)
XLA Ops:
  0.6 26.1 %shard_map.230 = (f32[224,384]{1,0:T(8,128)}, f32[24,512]{1,0:T(8,128)}) custom-call(f32[14,14,336]{2,1,0:T(8,128)} %residual.1, bf16[128,224]{1,0:T(8,128)(2,1)} %constant.44.clone.refs_0_, bf16[2,768,256]{2,1,0:T(8,128)(2,1)} %constant.45.clone.refs_1_, bf16[400,672]{1,0:T(8,128)(2,1)} %constant.46.clone.refs_2_, bf16[16,672]{1,0:T(8,128)(2,1)} %constant.47.clone.refs_3_, ...), custom_call_target="tpu_custom_call" | custom-call | flops 1000000000 | bytes 10000000 | tf_op jit(solution)/shard_map/pallas_call | solution.py:682
  26.7 1.9 %shard_map.231 = (f32[14,14,336]{2,1,0:T(8,128)}, f32[2,2,48]{2,1,0:T(2,128)}) custom-call(bf16[224,72]{1,0:T(8,128)(2,1)} %constant.65.clone.spread, f32[224,384]{1,0:T(8,128)} %get-tuple-element.4.total, f32[24,512]{1,0:T(8,128)} %get-tuple-element.5.nodes), custom_call_target="tpu_custom_call" | custom-call | flops 10000000 | bytes 1000000 | tf_op jit(solution)/shard_map/pallas_call | solution.py:718

commit v6 on v5

--- a/solution.py
+++ b/solution.py
@@ -479,14 +479,20 @@
     in_b[...] = jnp.zeros_like(in_b)
     in_d[...] = jnp.zeros_like(in_d)
     barrier = pltpu.get_barrier_semaphore()
-    for o in range(1, mesh_x):
-        pl.semaphore_signal(
-            barrier, inc=1, device_id=(lax.rem(ix + o, mesh_x), iy), device_id_type=MESH
-        )
-    for o in range(1, mesh_y):
-        pl.semaphore_signal(
-            barrier, inc=1, device_id=(ix, lax.rem(iy + o, mesh_y)), device_id_type=MESH
-        )
+
+    def greet_x(o):
+        to = lax.rem(ix + o, mesh_x)
+        pl.semaphore_signal(barrier, inc=1, device_id=(to, iy), device_id_type=MESH)
+
+    def greet_y(o):
+        to = lax.rem(iy + o, mesh_y)
+        pl.semaphore_signal(barrier, inc=1, device_id=(ix, to), device_id_type=MESH)
+
+    near_x, near_y = sorted({1, mesh_x - 1}), sorted({1, mesh_y - 1})
+    for o in near_y:
+        greet_y(o)
+    for o in near_x:
+        greet_x(o)
     corners = DIRECTIONS[4:]
     for dx, dy in corners:
         @pl.when(exists(dx, dy))
@@ -494,6 +500,10 @@
             pl.semaphore_signal(barrier, inc=1, device_id=(ix + dx, iy + dy), device_id_type=MESH)
 
     start_of_grid = 2 * (ix == 0).astype(jnp.int32) + (iy == 0).astype(jnp.int32)
+    for o in range(2, mesh_y - 1):
+        greet_y(o)
+    for o in range(2, mesh_x - 1):
+        greet_x(o)
     own[...] = jnp.zeros_like(own)
     place_x = 1 - (ix == 0).astype(jnp.int32) + (ix == mesh_x - 1).astype(jnp.int32)
     place_y = 1 - (iy == 0).astype(jnp.int32) + (iy == mesh_y - 1).astype(jnp.int32)
@@ -575,13 +585,15 @@
     first = first * (keep * (1.0 / theta_cheb))
     z_lap = table("z_lap")
     coefs = coefs - left_two(table("lap_own"), to_coefs(first, z_lap, windows))
-    arrived(copies_d)
-    coefs = coefs - left_two(table("lap_halo"), to_coefs(in_d[...], z_lap, windows))
     sigma = theta_cheb / delta_cheb
     rho_0 = 1.0 / sigma
     rho_1 = 1.0 / (2.0 * sigma - rho_0)
     weight_0, weight_1 = (1.0 + rho_1 * rho_0) / theta_cheb, 2.0 * rho_1 / delta_cheb
-    modes = weight_0 * modes_0 + weight_1 * (coefs * table("inverse"))
+    inverse = weight_1 * table("inverse")
+    modes = weight_0 * modes_0 + coefs * inverse
+    arrived(copies_d)
+    rest = left_two(table("lap_halo"), to_coefs(in_d[...], z_lap, windows))
+    modes = modes - rest * inverse
 
     lanes = dims["lanes"]
     shares = left(table("coarse_m"), modes)

time: 28.8 us -> 28.7 us (level)
  no operation moved by 1% of the time
where the time goes in v6:
time: 28.7 us; the launch traced here: 28.5 us
  Pallas kernels  27.9 us (97%)
  between operations  0.64 us (2%)
    pallas_call x1, Pallas kernels, per_device(): pl.pallas_call(functools.partial(kernel, names, dims, mesh_x, mesh_y), ou...  26 us
    pallas_call x1, Pallas kernels, per_device(): pl.pallas_call(functools.partial(finish, dims), out_shape=(jax.ShapeDtype...  1.91 us

profile of v6, /device:TPU:0, one launch (start us, length us, event | category | flops | bytes accessed | tf_op | source)
XLA Modules:
  0.0 28.5 jit_solution(366774396243003637)
XLA Ops:
  0.6 26.0 %shard_map.230 = (f32[224,384]{1,0:T(8,128)}, f32[24,512]{1,0:T(8,128)}) custom-call(f32[14,14,336]{2,1,0:T(8,128)} %residual.1, bf16[128,224]{1,0:T(8,128)(2,1)} %constant.44.clone.refs_0_, bf16[2,768,256]{2,1,0:T(8,128)(2,1)} %constant.45.clone.refs_1_, bf16[400,672]{1,0:T(8,128)(2,1)} %constant.46.clone.refs_2_, bf16[16,672]{1,0:T(8,128)(2,1)} %constant.47.clone.refs_3_, ...), custom_call_target="tpu_custom_call" | custom-call | flops 1000000000 | bytes 10000000 | tf_op jit(solution)/shard_map/pallas_call | solution.py:694
  26.6 1.9 %shard_map.231 = (f32[14,14,336]{2,1,0:T(8,128)}, f32[2,2,48]{2,1,0:T(2,128)}) custom-call(bf16[224,72]{1,0:T(8,128)(2,1)} %constant.65.clone.spread, f32[224,384]{1,0:T(8,128)} %get-tuple-element.4.total, f32[24,512]{1,0:T(8,128)} %get-tuple-element.5.nodes), custom_call_target="tpu_custom_call" | custom-call | flops 10000000 | bytes 1000000 | tf_op jit(solution)/shard_map/pallas_call | solution.py:730

commit v7 on v5

--- a/solution.py
+++ b/solution.py
@@ -505,7 +505,7 @@
         src = far[name].at[place[name]] if name in place else far[name]
         loads[name] = pltpu.make_async_copy(src, near[name], loaded.at[n])
 
-    later = names.index("back")
+    later = names.index("w_own")
     for name in names[:later]:
         loads[name].start()
 

time: 28.8 us -> 28.8 us (level)
  no operation moved by 1% of the time
where the time goes in v7:
time: 28.8 us; the launch traced here: 28.6 us
  Pallas kernels  28 us (97%)
  between operations  0.64 us (2%)
    pallas_call x1, Pallas kernels, per_device(): pl.pallas_call(functools.partial(kernel, names, dims, mesh_x, mesh_y), ou...  26.1 us
    pallas_call x1, Pallas kernels, per_device(): pl.pallas_call(functools.partial(finish, dims), out_shape=(jax.ShapeDtype...  1.91 us

profile of v7, /device:TPU:0, one launch (start us, length us, event | category | flops | bytes accessed | tf_op | source)
XLA Modules:
  0.0 28.6 jit_solution(11724722449921636685)
XLA Ops:
  0.6 26.1 %shard_map.230 = (f32[224,384]{1,0:T(8,128)}, f32[24,512]{1,0:T(8,128)}) custom-call(f32[14,14,336]{2,1,0:T(8,128)} %residual.1, bf16[128,224]{1,0:T(8,128)(2,1)} %constant.44.clone.refs_0_, bf16[2,768,256]{2,1,0:T(8,128)(2,1)} %constant.45.clone.refs_1_, bf16[400,672]{1,0:T(8,128)(2,1)} %constant.46.clone.refs_2_, bf16[16,672]{1,0:T(8,128)(2,1)} %constant.47.clone.refs_3_, ...), custom_call_target="tpu_custom_call" | custom-call | flops 1000000000 | bytes 10000000 | tf_op jit(solution)/shard_map/pallas_call | solution.py:682
  26.7 1.9 %shard_map.231 = (f32[14,14,336]{2,1,0:T(8,128)}, f32[2,2,48]{2,1,0:T(2,128)}) custom-call(bf16[224,72]{1,0:T(8,128)(2,1)} %constant.65.clone.spread, f32[224,384]{1,0:T(8,128)} %get-tuple-element.4.total, f32[24,512]{1,0:T(8,128)} %get-tuple-element.5.nodes), custom_call_target="tpu_custom_call" | custom-call | flops 10000000 | bytes 1000000 | tf_op jit(solution)/shard_map/pallas_call | solution.py:718
